TPU v7x, 32 devices: a whole 2x2x4 slice. The times are simulated.
32 devices in a mesh: expert: 16 (over z, y, x), shard: 2 (over core).
Axes of the slice: x: 2, y: 2, z: 4, core: 2. Of those that a mesh axis runs over, the one named last changes fastest.
Arguments:
- tokens: bfloat16 [8192, 768], P(('expert', 'shard')), may hold values from -6 to 6
- out_grad: bfloat16 [8192, 768], P(('expert', 'shard')), may hold values from -6 to 6
- seq_lengths: int32 [16, 4], P('expert'), may hold values from 1 to 384, 512 in all within a row
- expert_ids: int32 [8192, 1], P(('expert', 'shard')), may hold values from 0 to 15; in each aligned block of 256 rows (0 to 255, 256 to 511, ...) at most 32 rows name the same one
- w_query: bfloat16 [768, 768], P('shard'), may hold values from -0.21875 to 0.21875
- w_key: bfloat16 [768, 768], P('shard'), may hold values from -0.21875 to 0.21875
- w_value: bfloat16 [768, 768], P('shard'), may hold values from -0.21875 to 0.21875
- w_output: bfloat16 [768, 768], P('shard'), may hold values from -3 to 3
- w_router: bfloat16 [768, 16], P('shard'), may hold values from -0.15625 to 0.15625
- gain_attn: bfloat16 [768], P('shard'), may hold values from 0.5 to 1.5
- gain_ffn: bfloat16 [768], P('shard'), may hold values from 0.5 to 1.5
- bias_table: bfloat16 [32, 12], P('shard'), may hold values from -5 to 5
- expert_in: bfloat16 [16, 768, 3072], P('expert', None, 'shard'), may hold values from -0.21875 to 0.21875
- expert_out: bfloat16 [16, 3072, 768], P('expert', 'shard'), may hold values from -6 to 6
Outputs:
- layer_out: bfloat16 [8192, 768], P(('expert', 'shard'))
- grad_tokens: float32 [8192, 768], P(('expert', 'shard'))
- grad_w_query: float32 [768, 768], P('shard')
- grad_w_key: float32 [768, 768], P('shard')
- grad_w_value: float32 [768, 768], P('shard')
- grad_w_output: float32 [768, 768], P('shard')
- grad_w_router: float32 [768, 16], P('shard')
- grad_gain_attn: float32 [768], P('shard')
- grad_gain_ffn: float32 [768], P('shard')
- grad_bias_table: float32 [32, 12], P('shard')
- grad_expert_in: float32 [16, 768, 3072], P('expert', None, 'shard')
- grad_expert_out: float32 [16, 3072, 768], P('expert', 'shard')
Inputs may be any that keep to these rules, and one draw needn't show every extreme that they name: `seq_lengths`: row c lays its sequences end to end over the 512 tokens of group c; each row sums to 512 and its largest entry is exactly 384. `expert_ids`: among the 256 tokens of one device no expert is named more than 32 times, a bound that some block reaches.
All inputs are finite; a program needn't handle non-finite values.
Results may differ from a plain program's by a relative error of at most 0.014.
The roundings to bfloat16 on the way count: a program that leaves them out, or rounds other values in their place, can miss the bound.
Values may be sent and summed in bfloat16 or wider, within the bound.
A program may use at most 128 MiB of HBM per device.

v0:
```python
import jax
import jax.numpy as jnp
from jax import lax
from jax.sharding import PartitionSpec as P

bucket_edges = (8, 12, 16, 23, 32, 46, 64, 91)
epsilon = 1e-06
score_scale = 0.125
masked_score = -1e30
highest = lax.Precision.HIGHEST


def bucket_of(offsets):
    distance = jnp.abs(offsets)
    far_bucket = 8 + sum(
        ((distance >= boundary).astype(jnp.int32) for boundary in bucket_edges[1:])
    )
    near_bucket = jnp.where(distance < 8, distance, far_bucket)
    return near_bucket + 16 * (offsets > 0).astype(jnp.int32)


def bucket_onehot(query_places, key_places, bucket_count):
    offsets = key_places[None, :] - query_places[:, None]
    levels = jnp.arange(bucket_count, dtype=jnp.int32)
    return (bucket_of(offsets)[:, :, None] == levels[None, None, :]).astype(jnp.float32)


def rms_forward(hidden, gain_value):
    scale = lax.rsqrt(jnp.mean(hidden * hidden, axis=-1, keepdims=True) + epsilon)
    return (hidden * scale * gain_value, scale)


def rms_backward(hidden, scale, gain_value, grad_normed):
    weighted = grad_normed * gain_value
    grad_gain = jnp.sum(grad_normed * hidden * scale, axis=0)
    grad_hidden = scale * weighted - hidden * (scale * scale * scale) * jnp.mean(
        weighted * hidden, axis=-1, keepdims=True
    )
    return (grad_hidden, grad_gain)


def score_block(query_part, key_part, table_part, bucket_hot, query_docs, key_docs):
    raw_scores = (
        jnp.einsum("rhd,khd->hrk", query_part, key_part, preferred_element_type=jnp.float32)
        * score_scale
    )
    biased = raw_scores + jnp.einsum("rkb,hb->hrk", bucket_hot, table_part, precision=highest)
    same_doc = query_docs[:, None] == key_docs[None, :]
    return jnp.where(same_doc[None], biased, masked_score)


def attend_forward(
    query_heads,
    key_heads,
    value_heads,
    table_heads,
    query_places,
    query_docs,
    key_places,
    key_docs,
    head_group,
    block_rows,
):
    row_count, local_heads = (query_heads.shape[0], query_heads.shape[1])
    bucket_count = table_heads.shape[1]
    row_slice = slice(0, block_rows)
    bucket_hot = bucket_onehot(query_places, key_places, bucket_count)
    head_outputs = []
    lse_heads = []
    for head_first in range(0, local_heads, head_group):
        head_slice = slice(head_first, head_first + head_group)
        scores = score_block(
            query_heads[row_slice, head_slice],
            key_heads[:, head_slice],
            table_heads[head_slice],
            bucket_hot,
            query_docs,
            key_docs,
        )
        row_max = jnp.max(scores, axis=-1, keepdims=True)
        weights = jnp.exp(scores - row_max)
        row_total = jnp.sum(weights, axis=-1, keepdims=True)
        lse_heads.append(row_max + jnp.log(row_total))
        prob_low = (weights / row_total).astype(jnp.bfloat16)
        head_outputs.append(
            jnp.einsum(
                "hrk,khd->rhd",
                prob_low,
                value_heads[:, head_slice],
                preferred_element_type=jnp.float32,
            )
        )
    row_outputs = jnp.concatenate(head_outputs, axis=1)
    lse_blocks = [lse_heads]
    return (row_outputs, lse_blocks)


def attend_backward(
    query_heads,
    key_heads,
    value_heads,
    table_heads,
    query_places,
    query_docs,
    key_places,
    key_docs,
    head_group,
    block_rows,
    grad_attn_heads,
    lse_blocks,
):
    row_count, local_heads, head_size = query_heads.shape
    key_count = key_heads.shape[0]
    bucket_count = table_heads.shape[1]
    group_starts = list(range(0, local_heads, head_group))
    key_sums = [
        jnp.zeros((key_count, head_group, head_size), jnp.float32) for start in group_starts
    ]
    value_sums = [
        jnp.zeros((key_count, head_group, head_size), jnp.float32) for start in group_starts
    ]
    table_sums = [jnp.zeros((head_group, bucket_count), jnp.float32) for start in group_starts]
    query_rows = []
    for block_number, row_start in enumerate(range(0, row_count, block_rows)):
        row_slice = slice(row_start, row_start + block_rows)
        bucket_hot = bucket_onehot(query_places, key_places, bucket_count)
        query_heads_out = []
        for group_number, head_first in enumerate(group_starts):
            head_slice = slice(head_first, head_first + head_group)
            key_part = key_heads[:, head_slice]
            value_part = value_heads[:, head_slice]
            query_part = query_heads[row_slice, head_slice]
            scores = score_block(
                query_part, key_part, table_heads[head_slice], bucket_hot, query_docs, key_docs
            )
            probabilities = jnp.exp(scores - lse_blocks[block_number][group_number])
            grad_attn_part = grad_attn_heads[row_slice, head_slice]
            grad_probs = jnp.einsum(
                "rhd,khd->hrk", grad_attn_part, value_part, preferred_element_type=jnp.float32
            )
            row_dot = jnp.sum(probabilities * grad_probs, axis=-1, keepdims=True)
            grad_scores = probabilities * (grad_probs - row_dot)
            table_sums[group_number] = jnp.einsum(
                "hrk,rkb->hb", grad_scores, bucket_hot, precision=highest
            )
            grad_low = grad_scores.astype(jnp.bfloat16)
            query_heads_out.append(
                jnp.einsum("hrk,khd->rhd", grad_low, key_part, preferred_element_type=jnp.float32)
                * score_scale
            )
            key_sums[group_number] = (
                jnp.einsum("hrk,rhd->khd", grad_low, query_part, preferred_element_type=jnp.float32)
                * score_scale
            )
            value_sums[group_number] = jnp.einsum(
                "hrk,rhd->khd",
                probabilities.astype(jnp.bfloat16),
                grad_attn_part,
                preferred_element_type=jnp.float32,
            )
        query_rows.append(jnp.concatenate(query_heads_out, axis=1))
    grad_queries = query_rows[0].reshape(row_count, -1)
    grad_keys = jnp.concatenate(key_sums, axis=1).reshape(key_count, -1)
    grad_values = jnp.concatenate(value_sums, axis=1).reshape(key_count, -1)
    return (grad_queries, grad_keys, grad_values, jnp.concatenate(table_sums, axis=0))


def on_device(
    tokens,
    out_grad,
    seq_lengths,
    expert_ids,
    w_query,
    w_key,
    w_value,
    w_output,
    w_router,
    gain_attn,
    gain_ffn,
    bias_table,
    expert_in,
    expert_out,
):
    tok_count, model_width = tokens.shape
    experts = w_router.shape[1]
    capacity = 2 * tok_count // experts
    head_count = bias_table.shape[1]
    head_size = w_query.shape[1] // head_count
    block_rows = min(512, tok_count)
    head_group = max(1, head_count // 2)
    shard_count = lax.axis_size("shard")
    shard_index = lax.axis_index("shard")
    gathered = (
        lax.all_gather(w_query, "shard", axis=0, tiled=True),
        lax.all_gather(w_key, "shard", axis=0, tiled=True),
        lax.all_gather(w_value, "shard", axis=0, tiled=True),
        lax.all_gather(w_output, "shard", axis=0, tiled=True),
        lax.all_gather(w_router, "shard", axis=0, tiled=True),
        lax.all_gather(gain_attn, "shard", axis=0, tiled=True),
        lax.all_gather(gain_ffn, "shard", axis=0, tiled=True),
        lax.all_gather(bias_table, "shard", axis=0, tiled=True),
    )
    query_weight = gathered[0]
    key_weight = gathered[1]
    value_weight = gathered[2]
    output_weight = gathered[3]
    router_float = gathered[4].astype(jnp.float32)
    gain_one = gathered[5].astype(jnp.float32)
    gain_two = gathered[6].astype(jnp.float32)
    table_heads = gathered[7].astype(jnp.float32).T
    x_float = tokens.astype(jnp.float32)
    normed_one, scale_one = rms_forward(x_float, gain_one)
    normed_low = normed_one.astype(jnp.bfloat16)
    queries = jnp.dot(normed_low, query_weight, preferred_element_type=jnp.float32).astype(
        jnp.bfloat16
    )
    keys_local = jnp.dot(normed_low, key_weight, preferred_element_type=jnp.float32).astype(
        jnp.bfloat16
    )
    values_local = jnp.dot(normed_low, value_weight, preferred_element_type=jnp.float32).astype(
        jnp.bfloat16
    )
    keys_all, values_all = (
        lax.all_gather(keys_local, "shard", axis=0, tiled=True),
        lax.all_gather(values_local, "shard", axis=0, tiled=True),
    )
    query_places = shard_index * tok_count + jnp.arange(tok_count, dtype=jnp.int32)
    key_count = keys_all.shape[0]
    head_group = min(head_group, head_count)
    query_heads = queries.reshape(tok_count, head_count, head_size)
    key_heads = keys_all.reshape(key_count, head_count, head_size)
    value_heads = values_all.reshape(key_count, head_count, head_size)
    seq_ends = jnp.cumsum(seq_lengths[0])[:-1]
    key_places = jnp.arange(key_count, dtype=jnp.int32)
    key_docs = jnp.sum((key_places[:, None] >= seq_ends[None, :]).astype(jnp.int32), axis=1)
    query_docs = jnp.sum((query_places[:, None] >= seq_ends[None, :]).astype(jnp.int32), axis=1)
    attended, lse_blocks = attend_forward(
        query_heads,
        key_heads,
        value_heads,
        table_heads,
        query_places,
        query_docs,
        key_places,
        key_docs,
        head_group,
        block_rows,
    )
    attn_part = attended.reshape(tok_count, head_count * head_size).astype(jnp.bfloat16)
    hidden_one = x_float + jnp.dot(attn_part, output_weight, preferred_element_type=jnp.float32)
    normed_two, scale_two = rms_forward(hidden_one, gain_two)
    logits = jnp.dot(normed_two, router_float, precision=highest)
    route_probs = jax.nn.softmax(logits, axis=-1)
    route_flat = expert_ids[:, 0]
    expert_range = jnp.arange(experts, dtype=jnp.int32)
    route_int = (route_flat[:, None] == expert_range[None, :]).astype(jnp.int32)
    route_hot = route_int.astype(jnp.float32)
    gate_value = jnp.sum(route_probs * route_hot, axis=1)
    slot_ranks = jnp.sum(jnp.cumsum(route_int, axis=0) * route_int, axis=1) - 1
    slot_ids = route_flat * capacity + slot_ranks
    expert_low = normed_two.astype(jnp.bfloat16)
    send_rows = (
        jnp.zeros((experts * capacity, model_width), jnp.bfloat16).at[slot_ids].set(expert_low)
    )
    received = lax.all_to_all(
        send_rows.reshape(experts, capacity, model_width),
        "expert",
        split_axis=0,
        concat_axis=0,
        tiled=True,
    )
    expert_rows = lax.all_gather(received, "shard", axis=0, tiled=True).reshape(-1, model_width)
    weight_in = expert_in[0]
    weight_out = expert_out[0]
    pre_act = jnp.dot(expert_rows, weight_in, preferred_element_type=jnp.float32)
    act_low = jax.nn.gelu(pre_act).astype(jnp.bfloat16)
    expert_result = jnp.dot(act_low, weight_out, preferred_element_type=jnp.float32)
    expert_result = lax.psum_scatter(
        expert_result.reshape(shard_count * experts, capacity, model_width).astype(jnp.bfloat16),
        "shard",
        scatter_dimension=0,
        tiled=True,
    ).astype(jnp.float32)
    returned = lax.all_to_all(
        expert_result.astype(jnp.bfloat16), "expert", split_axis=0, concat_axis=0, tiled=True
    )
    result_float = returned.reshape(-1, model_width)[slot_ids].astype(jnp.float32)
    layer_out = (hidden_one + gate_value[:, None] * result_float).astype(jnp.bfloat16)
    grad_out = out_grad.astype(jnp.float32)
    grad_gate = jnp.sum(grad_out * result_float, axis=1)
    grad_result = (gate_value[:, None] * grad_out).astype(jnp.bfloat16)
    grad_send = (
        jnp.zeros((experts * capacity, model_width), jnp.bfloat16).at[slot_ids].set(grad_result)
    )
    grad_received = lax.all_to_all(
        grad_send.reshape(experts, capacity, model_width),
        "expert",
        split_axis=0,
        concat_axis=0,
        tiled=True,
    )
    grad_rows = lax.all_gather(grad_received, "shard", axis=0, tiled=True).reshape(-1, model_width)
    grad_act = jnp.einsum("rd,fd->rf", grad_rows, weight_out, preferred_element_type=jnp.float32)
    grad_w_out = jnp.einsum("rf,rd->fd", act_low, grad_rows, preferred_element_type=jnp.float32)
    gelu_value, gelu_pull = jax.vjp(jax.nn.gelu, pre_act)
    grad_pre = gelu_pull(grad_act)[0].astype(jnp.bfloat16)
    grad_w_in = jnp.einsum("rd,rf->df", expert_rows, grad_pre, preferred_element_type=jnp.float32)
    grad_rows_in = jnp.einsum("rf,df->rd", grad_pre, weight_in, preferred_element_type=jnp.float32)
    grad_rows_in = lax.psum_scatter(
        grad_rows_in.reshape(shard_count * experts, capacity, model_width).astype(jnp.bfloat16),
        "shard",
        scatter_dimension=0,
        tiled=True,
    ).astype(jnp.float32)
    grad_back = lax.all_to_all(
        grad_rows_in.astype(jnp.bfloat16), "expert", split_axis=0, concat_axis=0, tiled=True
    )
    grad_expert_tok = grad_back.reshape(-1, model_width)[slot_ids].astype(jnp.float32)
    grad_logits = gate_value[:, None] * (route_hot - route_probs) * grad_gate[:, None]
    grad_router = jnp.einsum("td,te->de", normed_two, grad_logits, precision=highest)
    grad_normed_two = (
        jnp.einsum("te,de->td", grad_logits, router_float, precision=highest) + grad_expert_tok
    )
    grad_hidden_norm, grad_gain_two = rms_backward(hidden_one, scale_two, gain_two, grad_normed_two)
    grad_hidden = grad_out + grad_hidden_norm
    grad_branch = grad_hidden.astype(jnp.bfloat16)
    grad_w_output = jnp.einsum(
        "tc,td->cd", attn_part, grad_branch, preferred_element_type=jnp.float32
    )
    grad_attn = jnp.einsum(
        "td,cd->tc", grad_branch, output_weight, preferred_element_type=jnp.float32
    ).astype(jnp.bfloat16)
    grad_attn_heads = grad_attn.reshape(tok_count, head_count, head_size)
    grad_q_part, grad_k_part, grad_v_part, table_part = attend_backward(
        query_heads,
        key_heads,
        value_heads,
        table_heads,
        query_places,
        query_docs,
        key_places,
        key_docs,
        head_group,
        block_rows,
        grad_attn_heads,
        lse_blocks,
    )
    grad_queries = grad_q_part.astype(jnp.bfloat16)
    grad_keys_mine, grad_values_mine = (
        lax.psum_scatter(
            grad_k_part.astype(jnp.bfloat16), "shard", scatter_dimension=0, tiled=True
        ).astype(jnp.float32),
        lax.psum_scatter(
            grad_v_part.astype(jnp.bfloat16), "shard", scatter_dimension=0, tiled=True
        ).astype(jnp.float32),
    )
    grad_keys = grad_keys_mine.astype(jnp.bfloat16)
    grad_values = grad_values_mine.astype(jnp.bfloat16)
    grad_table = table_part.T
    grad_w_query = jnp.einsum(
        "td,tc->dc", normed_low, grad_queries, preferred_element_type=jnp.float32
    )
    grad_w_key = jnp.einsum("td,tc->dc", normed_low, grad_keys, preferred_element_type=jnp.float32)
    grad_w_value = jnp.einsum(
        "td,tc->dc", normed_low, grad_values, preferred_element_type=jnp.float32
    )
    grad_normed_one = jnp.einsum(
        "tc,dc->td", grad_queries, query_weight, preferred_element_type=jnp.float32
    )
    grad_normed_one = grad_normed_one + jnp.einsum(
        "tc,dc->td", grad_keys, key_weight, preferred_element_type=jnp.float32
    )
    grad_normed_one = grad_normed_one + jnp.einsum(
        "tc,dc->td", grad_values, value_weight, preferred_element_type=jnp.float32
    )
    grad_x_norm, grad_gain_one = rms_backward(x_float, scale_one, gain_one, grad_normed_one)
    grad_tokens = grad_hidden + grad_x_norm
    totals = lax.psum(
        (
            grad_w_query,
            grad_w_key,
            grad_w_value,
            grad_w_output,
            grad_router,
            grad_gain_one,
            grad_gain_two,
            grad_table,
        ),
        ("expert", "shard"),
    )

    def own_half(whole):
        half_rows = whole.shape[0] // shard_count
        return lax.dynamic_slice_in_dim(whole, shard_index * half_rows, half_rows, 0)

    grad_expert_in = grad_w_in[None]
    grad_expert_out = grad_w_out[None]
    return (
        layer_out,
        grad_tokens,
        own_half(totals[0]),
        own_half(totals[1]),
        own_half(totals[2]),
        own_half(totals[3]),
        own_half(totals[4]),
        own_half(totals[5]),
        own_half(totals[6]),
        own_half(totals[7]),
        grad_expert_in,
        grad_expert_out,
    )


def solution(mesh):
    placed = (
        P(("expert", "shard"), None),
        P(("expert", "shard"), None),
        P("expert", None),
        P(("expert", "shard"), None),
        P("shard", None),
        P("shard", None),
        P("shard", None),
        P("shard", None),
        P("shard", None),
        P("shard"),
        P("shard"),
        P("shard", None),
        P("expert", None, "shard"),
        P("expert", "shard", None),
    )
    return jax.shard_map(
        on_device,
        mesh=mesh,
        in_specs=placed,
        out_specs=(
            P(("expert", "shard"), None),
            P(("expert", "shard"), None),
            P("shard", None),
            P("shard", None),
            P("shard", None),
            P("shard", None),
            P("shard", None),
            P("shard"),
            P("shard"),
            P("shard", None),
            P("expert", None, "shard"),
            P("expert", "shard", None),
        ),
        check_vma=False,
    )
```

profile of v0, /device:TPU:0, one launch (start us, length us, event | category | flops | bytes accessed | tf_op | source)
XLA Modules:
  0.0 455.6 jit_solution(7900403015264150017)
XLA Ops:
  11.6 2.1 all_gather.42
  13.7 4.6 %fusion.3 = f32[256,512,6]{0,2,1:T(8,128)} fusion(s32[256,512]{0,1:T(8,128)S(1)} %fusion.91, bf16[12,32]{1,0:T(8,128)(2,1)S(1)} %bitcast.173), kind=kOutput, calls=%fused_computation.8 | convolution fusion | flops 54525952 | bytes 3672064 | tf_op jit(solution)/shard_map/rkb,hb->hrk/dot_general | solution.py:47
  18.3 4.6 %fusion.2 = f32[256,512,6]{0,2,1:T(8,128)} fusion(s32[256,512]{0,1:T(8,128)S(1)} %fusion.91, bf16[12,32]{1,0:T(8,128)(2,1)S(1)} %bitcast.174), kind=kOutput, calls=%fused_computation.7 | convolution fusion | flops 54525952 | bytes 3672064 | tf_op jit(solution)/shard_map/rkb,hb->hrk/dot_general | solution.py:47
  25.5 4.9 %copy.71 = f32[256,512,6]{1,0,2:T(8,128)} copy(f32[256,512,6]{0,2,1:T(8,128)} %fusion.3) | data formatting | bytes 6291456 | tf_op jit(solution)/shard_map/rkb,hb->hrk/dot_general | solution.py:47
  30.4 5.0 %copy.72 = f32[256,512,6]{1,0,2:T(8,128)} copy(f32[256,512,6]{0,2,1:T(8,128)} %fusion.2) | data formatting | bytes 6291456 | tf_op jit(solution)/shard_map/rkb,hb->hrk/dot_general | solution.py:47
  38.9 1.8 convolution_convert_fusion.1
  40.7 2.4 all_gather.41
  44.2 1.8 convolution_convert_fusion.2
  46.9 1.8 convolution_convert_fusion.3
  48.7 2.5 all_gather.38
  52.4 3.5 fusion.146
  62.5 2.0 multiply_reduce_fusion.4
  65.1 2.7 scatter_custom_fusion
  67.7 8.4 %all-to-all-start = ((bf16[16,32,768]{2,1,0:T(8,128)(2,1)}), bf16[16,32,768]{2,1,0:T(8,128)(2,1)}, u32[]{:S(2)}, u32[]{:S(2)}) async-start(bf16[16,32,768]{2,1,0:T(8,128)(2,1)} %bitcast.147), calls=%async_computation | async-start | bytes 1572864 | tf_op jit(solution)/shard_map/all_to_all | solution.py:265
  76.3 2.2 all_gather.45
  81.6 14.7 %all-to-all-done = bf16[16,32,768]{2,1,0:T(8,128)(2,1)} async-done(((bf16[16,32,768]{2,1,0:T(8,128)(2,1)}), bf16[16,32,768]{2,1,0:T(8,128)(2,1)}, u32[]{:S(2)}, u32[]{:S(2)}) %all-to-all-start) | async-done | bytes 786464 | tf_op jit(solution)/shard_map/all_to_all | solution.py:265
  97.6 3.1 scatter_custom_fusion.1
  100.7 25.3 %all_to_all.20 = bf16[16,32,768]{2,1,0:T(8,128)(2,1)} all-to-all(bf16[16,32,768]{2,1,0:T(8,128)(2,1)} %bitcast.148), channel_id=1, replica_groups=mesh['expert'=16,'shard'=2] {'expert'}, dimensions={0} | all-to-all | bytes 1572864 | tf_op jit(solution)/shard_map/all_to_all | solution.py:295
  126.3 7.0 %multiply_convert_fusion = (bf16[1024,1536]{1,0:T(8,128)(2,1)}, f32[1024,1536]{1,0:T(8,128)}) fusion(bf16[1024,768]{1,0:T(8,128)(2,1)} %bitcast.150, bf16[1,768,1536]{2,1,0:T(8,128)(2,1)S(1)} %copy-done), kind=kOutput, calls=%fused_computation.22 | convolution fusion | flops 2430074880 | bytes 13369344 | tf_op jit(solution)/shard_map/dot_general | solution.py:275
  133.7 8.4 %fusion.14 = bf16[1024,1536]{1,0:T(8,128)(2,1)S(1)} fusion(f32[1024,1536]{1,0:T(8,128)} %get-tuple-element.87, bf16[1024,768]{1,0:T(8,128)(2,1)} %bitcast.179, bf16[1,1536,768]{2,1,0:T(8,128)(2,1)} %param.27), kind=kOutput, calls=%fused_computation.21 | convolution fusion | flops 2447376384 | bytes 13369344 | tf_op jit(solution)/shard_map/rd,fd->rf/dot_general | solution.py:303
  143.7 3.8 fusion.34
  147.6 6.4 %fusion.31 = bf16[32,32,768]{2,1,0:T(8,128)(2,1)} fusion(bf16[32,32,1536]{2,1,0:T(8,128)(2,1)} %bitcast.182, bf16[1,1536,768]{2,1,0:T(8,128)(2,1)} %param.27), kind=kOutput, calls=%fused_computation.57 | convolution fusion | flops 2416705536 | bytes 7077888 | tf_op jit(solution)/shard_map/dot_general | solution.py:277
  154.0 3.9 reduce-scatter.7.cloned.1.call-done
  157.9 6.8 %all-to-all-start.3 = ((bf16[16,32,768]{2,1,0:T(8,128)(2,1)}), bf16[16,32,768]{2,1,0:T(8,128)(2,1)S(1)}, u32[]{:S(2)}, u32[]{:S(2)}) async-start(bf16[16,32,768]{2,1,0:T(8,128)(2,1)} %reduce-scatter.7.cloned.1.call-done), calls=%async_computation.5 | async-start | bytes 1572864 | tf_op jit(solution)/shard_map/all_to_all | solution.py:315
  164.7 5.8 %reduce-scatter.5.cloned.1.call-done = bf16[16,32,768]{2,1,0:T(8,128)(2,1)} async-done(((bf16[32,32,768]{2,1,0:T(8,128)(2,1)}), bf16[16,32,768]{2,1,0:T(8,128)(2,1)}) %reduce-scatter.5.cloned.1.call-update) | async-done | bytes 786448 | tf_op jit(solution)/shard_map/reduce_scatter | solution.py:278
  170.5 14.3 %all-to-all-done.3 = bf16[16,32,768]{2,1,0:T(8,128)(2,1)S(1)} async-done(((bf16[16,32,768]{2,1,0:T(8,128)(2,1)}), bf16[16,32,768]{2,1,0:T(8,128)(2,1)S(1)}, u32[]{:S(2)}, u32[]{:S(2)}) %all-to-all-start.3) | async-done | bytes 786464 | tf_op jit(solution)/shard_map/all_to_all | solution.py:315
  184.8 5.0 %all-to-all-start.1 = ((bf16[16,32,768]{2,1,0:T(8,128)(2,1)}), bf16[16,32,768]{2,1,0:T(8,128)(2,1)S(1)}, u32[]{:S(2)}, u32[]{:S(2)}) async-start(bf16[16,32,768]{2,1,0:T(8,128)(2,1)} %reduce-scatter.5.cloned.1.call-done), calls=%async_computation.2 | async-start | bytes 1572864 | tf_op jit(solution)/shard_map/all_to_all | solution.py:284
  191.5 1.9 gather_fusion.1
  193.5 15.1 %all-to-all-done.1 = bf16[16,32,768]{2,1,0:T(8,128)(2,1)S(1)} async-done(((bf16[16,32,768]{2,1,0:T(8,128)(2,1)}), bf16[16,32,768]{2,1,0:T(8,128)(2,1)S(1)}, u32[]{:S(2)}, u32[]{:S(2)}) %all-to-all-start.1) | async-done | bytes 786464 | tf_op jit(solution)/shard_map/all_to_all | solution.py:284
  210.0 2.4 multiply_reduce_fusion.2
  212.4 2.1 convert_add_fusion.1
  215.2 5.4 %multiply_reduce_fusion.1 = (f32[6,256]{1,0:T(8,128)}, f32[6,256,512]{2,1,0:T(8,128)}) fusion(f32[6,256,512]{2,1,0:T(8,128)} %copy-done.9, f32[6,256]{1,0:T(8,128)} %log_add_fusion.1, bf16[256,12,64]{0,2,1:T(8,128)(2,1)S(1)} %bitcast.164, bf16[512,12,64]{0,2,1:T(8,128)(2,1)} %bitcast.156), kind=kOutput, calls=%fused_computation.33 | convolution fusion | flops 103021056 | bytes 7092224 | tf_op jit(solution)/shard_map/rhd,khd->hrk/dot_general | solution.py:138
  224.4 3.3 subtract_multiply_fusion.1
  228.2 2.6 copy-done.8
  236.3 2.6 fusion.66
  239.8 2.1 fusion.140
  241.9 2.0 fusion.120
  243.9 3.0 fusion.136
  246.9 3.1 fusion.138
  250.0 7.4 %convolution_bitcast_fusion = f32[1,1536,768]{2,1,0:T(8,128)} fusion(bf16[1024,1536]{1,0:T(8,128)(2,1)} %get-tuple-element.86, bf16[1024,768]{1,0:T(8,128)(2,1)} %bitcast.180), kind=kOutput, calls=%fused_computation.23 | convolution fusion | flops 2415919104 | bytes 9437184 | tf_op jit(solution)/shard_map/rf,rd->fd/dot_general | solution.py:304
  257.4 4.3 convolution_bitcast_fusion.1
  261.7 5.2 %copy.75 = f32[6,256,512]{1,0,2:T(8,128)} copy(f32[6,256,512]{2,1,0:T(8,128)} %copy-done.3) | data formatting | bytes 6291456 | tf_op jit(solution)/shard_map/mul | solution.py:142
  266.9 5.3 %copy.76 = f32[6,256,512]{1,0,2:T(8,128)} copy(f32[6,256,512]{2,1,0:T(8,128)} %copy-done.4) | data formatting | bytes 6291456 | tf_op jit(solution)/shard_map/mul | solution.py:142
  272.1 10.1 %fusion.69 = f32[6,32]{1,0:T(8,128)S(1)} fusion(f32[6,256,512]{1,0,2:T(8,128)} %copy.75, s32[256,512]{0,1:T(8,128)S(1)} %copy-done.12), kind=kOutput, calls=%fused_computation.96 | convolution fusion | flops 306184192 | bytes 3670784 | tf_op jit(solution)/shard_map/hrk,rkb->hb/dot_general | solution.py:143
  282.3 7.9 %fusion.70 = f32[6,32]{1,0:T(8,128)S(1)} fusion(f32[6,256,512]{1,0,2:T(8,128)S(1)} %copy-done.14, s32[256,512]{0,1:T(8,128)S(1)} %copy-done.12), kind=kOutput, calls=%fused_computation.97 | convolution fusion | flops 306184192 | bytes 3670784 | tf_op jit(solution)/shard_map/hrk,rkb->hb/dot_general | solution.py:143
  292.8 41.7 %all-reduce = (f32[768,16]{0,1:T(8,128)S(1)}, f32[768]{0:T(1024)S(1)}, f32[768]{0:T(1024)S(1)}, f32[32,12]{0,1:T(8,128)S(1)}) all-reduce(f32[768,16]{0,1:T(8,128)S(1)} %fusion.88, f32[768]{0:T(1024)S(1)} %get-tuple-element.62, f32[768]{0:T(1024)S(1)} %copy-done.64, ...), channel_id=1, replica_groups=mesh['expert'=16,'shard'=2] {'expert','shard'}, use_global_device_ids=true, to_apply=%region_30.31 | all-reduce | flops 14208 | bytes 113664 | tf_op jit(solution)/shard_map/psum | solution.py:378
  338.4 105.4 %all-reduce.4.cloned.1.call-done = (f32[768,768]{1,0:T(8,128)}, f32[768,768]{1,0:T(8,128)}, f32[768,768]{1,0:T(8,128)}, f32[768,768]{1,0:T(8,128)}) async-done(((f32[768,768]{1,0:T(8,128)}, f32[768,768]{1,0:T(8,128)}, f32[768,768]{1,0:T(8,128)}, f32[768,768]{1,0:T(8,128)}), (f32[768,768]{1,0:T(8,128)}, f32[768,768]{1,0:T(8,128)}, f32[768,768]{1,0:T(8,128)}, ...) | async-done | bytes 9437200 | tf_op jit(solution)/shard_map/psum | solution.py:378
  443.8 3.3 constant_dynamic-slice_fusion.2
  (245 shorter events, 49.8 us)
Async XLA Ops:
  7.2 119.1 %copy-start = (bf16[1,768,1536]{2,1,0:T(8,128)(2,1)S(1)}, bf16[1,768,1536]{2,1,0:T(8,128)(2,1)}, u32[]{:S(2)}) copy-start(bf16[1,768,1536]{2,1,0:T(8,128)(2,1)} %param.26) | copy-start | bytes 7077892
  7.2 31.7 %all-gather.13.cloned.1.call-start = ((), (), s32[]{:S(2)}) async-start(), calls=%async_computation.10 | async-start | bytes 1769472 | tf_op jit(solution)/shard_map/all_gather | solution.py:195
  7.9 36.3 %all-gather.11.cloned.1.call-start = ((), (), s32[]{:S(2)}) async-start(), calls=%async_computation.9 | async-start | bytes 1769472 | tf_op jit(solution)/shard_map/all_gather | solution.py:194
  8.7 38.2 %all-gather.9.cloned.1.call-start = ((), (), s32[]{:S(2)}) async-start(), calls=%async_computation.8 | async-start | bytes 1769472 | tf_op jit(solution)/shard_map/all_gather | solution.py:196
  9.4 53.1 %all-gather.15.cloned.1.call-start = ((), (), s32[]{:S(2)}) async-start(), calls=%async_computation.11 | async-start | bytes 1769472 | tf_op jit(solution)/shard_map/all_gather | solution.py:197
  10.5 12.3 %copy-start.11 = (s32[256,512]{0,1:T(8,128)}, s32[256,512]{0,1:T(8,128)S(1)}, u32[]{:S(2)}) copy-start(s32[256,512]{0,1:T(8,128)S(1)} %fusion.91) | copy-start | bytes 1572868
  18.3 5.3 %copy-start.71 = (bf16[384]{0:T(512)(128)(2,1)S(1)}, bf16[384]{0:T(512)(128)(2,1)}, u32[]{:S(2)}) copy-start(bf16[384]{0:T(512)(128)(2,1)} %param.23) | copy-start | bytes 2308
  23.6 23.3 %copy-start.44 = (f32[256]{0:T(256)}, f32[256]{0:T(256)S(1)}, u32[]{:S(2)}) copy-start(f32[256]{0:T(256)S(1)} %get-tuple-element.75) | copy-start | bytes 3076
  25.4 21.5 %copy-start.39 = (f32[768]{0:T(1024)}, f32[768]{0:T(1024)S(1)}, u32[]{:S(2)}) copy-start(f32[768]{0:T(1024)S(1)} %reshape.289) | copy-start | bytes 9220
  30.4 6.8 %copy-start.48 = (s32[256,1]{0,1:T(1,128)S(1)}, s32[256,1]{0,1:T(1,128)}, u32[]{:S(2)}) copy-start(s32[256,1]{0,1:T(1,128)} %param.17) | copy-start | bytes 3076
  37.1 28.0 %copy-start.41 = (f32[768]{0:T(1024)}, f32[768]{0:T(1024)S(1)}, u32[]{:S(2)}) copy-start(f32[768]{0:T(1024)S(1)} %reshape.290) | copy-start | bytes 9220
  38.1 27.0 %copy-start.69 = (s32[256,1]{0,1:T(1,128)}, s32[256,1]{0,1:T(1,128)S(1)}, u32[]{:S(2)}) copy-start(s32[256,1]{0,1:T(1,128)S(1)} %compare_select_fusion.1) | copy-start | bytes 3076
  65.1 11.2 %copy-start.46 = (f32[256]{0:T(256)}, f32[256]{0:T(256)S(1)}, u32[]{:S(2)}) copy-start(f32[256]{0:T(256)S(1)} %get-tuple-element.77) | copy-start | bytes 3076
  67.7 28.5 %all-to-all-start = ((bf16[16,32,768]{2,1,0:T(8,128)(2,1)}), bf16[16,32,768]{2,1,0:T(8,128)(2,1)}, u32[]{:S(2)}, u32[]{:S(2)}) async-start(bf16[16,32,768]{2,1,0:T(8,128)(2,1)} %bitcast.147), calls=%async_computation | async-start | bytes 1572864 | tf_op jit(solution)/shard_map/all_to_all | solution.py:265
  76.2 50.1 %all-gather.17.cloned.1.call-start = ((), (), s32[]{:S(2)}) async-start(), calls=%async_computation.12 | async-start | bytes 2359296 | tf_op jit(solution)/shard_map/all_gather | solution.py:272
  96.3 37.4 %all-gather.19.cloned.1.call-start = ((), (), s32[]{:S(2)}) async-start(), calls=%async_computation.14 | async-start | bytes 2359296 | tf_op jit(solution)/shard_map/all_gather | solution.py:302
  126.0 31.9 %reduce-scatter.7.cloned.1.call-start = ((), (), s32[]{:S(2)}) async-start(), calls=%async_computation.15 | async-start | bytes 2359296 | tf_op jit(solution)/shard_map/reduce_scatter | solution.py:309
  147.5 23.0 %reduce-scatter.5.cloned.1.call-start = ((), (), s32[]{:S(2)}) async-start(), calls=%async_computation.13 | async-start | bytes 2359296 | tf_op jit(solution)/shard_map/reduce_scatter | solution.py:278
  154.0 36.3 %copy-start.70 = (s32[256,1]{0,1:T(1,128)S(1)}, s32[256,1]{0,1:T(1,128)}, u32[]{:S(2)}) copy-start(s32[256,1]{0,1:T(1,128)} %copy-done.69) | copy-start | bytes 3076
  154.0 36.3 %copy-start.51 = (f32[6,256]{1,0:T(8,128)S(1)}, f32[6,256]{1,0:T(8,128)}, u32[]{:S(2)}) copy-start(f32[6,256]{1,0:T(8,128)} %copy-done.50) | copy-start | bytes 18436
  154.0 36.3 %copy-start.57 = (f32[6,256]{1,0:T(8,128)S(1)}, f32[6,256]{1,0:T(8,128)}, u32[]{:S(2)}) copy-start(f32[6,256]{1,0:T(8,128)} %copy-done.56) | copy-start | bytes 18436
  154.0 36.9 %copy-start.53 = (f32[6,256]{1,0:T(8,128)S(1)}, f32[6,256]{1,0:T(8,128)}, u32[]{:S(2)}) copy-start(f32[6,256]{1,0:T(8,128)} %copy-done.52) | copy-start | bytes 18436
  154.0 36.9 %copy-start.55 = (f32[6,256]{1,0:T(8,128)S(1)}, f32[6,256]{1,0:T(8,128)}, u32[]{:S(2)}) copy-start(f32[6,256]{1,0:T(8,128)} %copy-done.54) | copy-start | bytes 18436
  157.9 26.9 %all-to-all-start.3 = ((bf16[16,32,768]{2,1,0:T(8,128)(2,1)}), bf16[16,32,768]{2,1,0:T(8,128)(2,1)S(1)}, u32[]{:S(2)}, u32[]{:S(2)}) async-start(bf16[16,32,768]{2,1,0:T(8,128)(2,1)} %reduce-scatter.7.cloned.1.call-done), calls=%async_computation.5 | async-start | bytes 1572864 | tf_op jit(solution)/shard_map/all_to_all | solution.py:315
  184.8 23.8 %all-to-all-start.1 = ((bf16[16,32,768]{2,1,0:T(8,128)(2,1)}), bf16[16,32,768]{2,1,0:T(8,128)(2,1)S(1)}, u32[]{:S(2)}, u32[]{:S(2)}) async-start(bf16[16,32,768]{2,1,0:T(8,128)(2,1)} %reduce-scatter.5.cloned.1.call-done), calls=%async_computation.2 | async-start | bytes 1572864 | tf_op jit(solution)/shard_map/all_to_all | solution.py:284
  189.8 54.1 %reduce-scatter.11.cloned.1.call-start = ((), (), s32[]{:S(2)}) async-start(), calls=%async_computation.17 | async-start | bytes 1179648 | tf_op jit(solution)/shard_map/reduce_scatter | solution.py:353
  191.5 18.2 %copy-start.15 = (bf16[256,768]{1,0:T(8,128)(2,1)S(1)}, bf16[256,768]{1,0:T(8,128)(2,1)}, u32[]{:S(2)}) copy-start(bf16[256,768]{1,0:T(8,128)(2,1)} %param.15) | copy-start | bytes 1179652
  193.5 16.5 %copy-start.24 = (bf16[256,768]{1,0:T(8,128)(2,1)S(1)}, bf16[256,768]{1,0:T(8,128)(2,1)}, u32[]{:S(2)}) copy-start(bf16[256,768]{1,0:T(8,128)(2,1)} %gather_fusion.1) | copy-start | bytes 1179652
  215.2 6.2 %copy-start.36 = (bf16[256,768]{0,1:T(8,128)(2,1)}, bf16[256,768]{0,1:T(8,128)(2,1)S(1)}, u32[]{:S(2)}) copy-start(bf16[256,768]{0,1:T(8,128)(2,1)S(1)} %copy.74) | copy-start | bytes 1179652
  215.2 5.4 %copy-start.10 = (f32[6,256,512]{2,1,0:T(8,128)S(1)}, f32[6,256,512]{2,1,0:T(8,128)}, u32[]{:S(2)}) copy-start(f32[6,256,512]{2,1,0:T(8,128)} %copy-done.9) | copy-start | bytes 9437188
  215.2 5.4 %copy-start.60 = (f32[6,256]{1,0:T(8,128)S(1)}, f32[6,256]{1,0:T(8,128)}, u32[]{:S(2)}) copy-start(f32[6,256]{1,0:T(8,128)} %log_add_fusion.1) | copy-start | bytes 18436
  224.3 22.6 %reduce-scatter.9.cloned.1.call-start = ((), (), s32[]{:S(2)}) async-start(), calls=%async_computation.16 | async-start | bytes 1179648 | tf_op jit(solution)/shard_map/reduce_scatter | solution.py:350
  236.0 207.7 %all-reduce.4.cloned.1.call-start = ((), (), s32[]{:S(2)}) async-start(), calls=%async_computation.18 | async-start | bytes 18874368 | tf_op jit(solution)/shard_map/psum | solution.py:378
  250.0 7.4 %copy-start.20 = (bf16[1024,1536]{1,0:T(8,128)(2,1)S(1)}, bf16[1024,1536]{1,0:T(8,128)(2,1)}, u32[]{:S(2)}) copy-start(bf16[1024,1536]{1,0:T(8,128)(2,1)} %copy-done.19) | copy-start | bytes 9437188
  250.0 7.4 %copy-start.21 = (bf16[32,32,768]{2,1,0:T(8,128)(2,1)S(1)}, bf16[32,32,768]{2,1,0:T(8,128)(2,1)}, u32[]{:S(2)}) copy-start(bf16[32,32,768]{2,1,0:T(8,128)(2,1)} %all-gather.17.cloned.1.call-done) | copy-start | bytes 4718596
  266.9 5.3 %copy-start.12 = (s32[256,512]{0,1:T(8,128)S(1)}, s32[256,512]{0,1:T(8,128)}, u32[]{:S(2)}) copy-start(s32[256,512]{0,1:T(8,128)} %copy-done.11) | copy-start | bytes 1572868
  272.1 10.1 %copy-start.14 = (f32[6,256,512]{1,0,2:T(8,128)S(1)}, f32[6,256,512]{1,0,2:T(8,128)}, u32[]{:S(2)}) copy-start(f32[6,256,512]{1,0,2:T(8,128)} %copy.76) | copy-start | bytes 9437188
  282.2 8.0 %copy-start.42 = (f32[768]{0:T(1024)S(1)}, f32[768]{0:T(1024)}, u32[]{:S(2)}) copy-start(f32[768]{0:T(1024)} %copy-done.41) | copy-start | bytes 9220
  282.3 8.0 %copy-start.47 = (f32[256]{0:T(256)S(1)}, f32[256]{0:T(256)}, u32[]{:S(2)}) copy-start(f32[256]{0:T(256)} %copy-done.46) | copy-start | bytes 3076
  282.3 8.0 %copy-start.49 = (s32[256,1]{0,1:T(1,128)S(1)}, s32[256,1]{0,1:T(1,128)}, u32[]{:S(2)}) copy-start(s32[256,1]{0,1:T(1,128)} %param.17) | copy-start | bytes 3076
  282.3 8.0 %copy-start.61 = (f32[256]{0:T(256)S(1)}, f32[256]{0:T(256)}, u32[]{:S(2)}) copy-start(f32[256]{0:T(256)} %multiply_reduce_fusion.5) | copy-start | bytes 3076
  282.3 8.0 %copy-start.63 = (f32[256]{0:T(256)S(1)}, f32[256]{0:T(256)}, u32[]{:S(2)}) copy-start(f32[256]{0:T(256)} %copy-done.62) | copy-start | bytes 3076
  282.3 8.0 %copy-start.65 = (f32[256]{0:T(256)S(1)}, f32[256]{0:T(256)}, u32[]{:S(2)}) copy-start(f32[256]{0:T(256)} %fusion.127) | copy-start | bytes 3076
  282.3 8.0 %copy-start.67 = (f32[256]{0:T(256)S(1)}, f32[256]{0:T(256)}, u32[]{:S(2)}) copy-start(f32[256]{0:T(256)} %copy-done.66) | copy-start | bytes 3076
  282.3 8.7 %copy-start.27 = (bf16[768,768]{1,0:T(8,128)(2,1)S(1)}, bf16[768,768]{1,0:T(8,128)(2,1)}, u32[]{:S(2)}) copy-start(bf16[768,768]{1,0:T(8,128)(2,1)} %all-gather.11.cloned.1.call-done) | copy-start | bytes 3538948
  282.3 9.2 %copy-start.23 = (bf16[256,768]{0,1:T(8,128)(2,1)S(1)}, bf16[256,768]{0,1:T(8,128)(2,1)}, u32[]{:S(2)}) copy-start(bf16[256,768]{0,1:T(8,128)(2,1)} %reduce-scatter.9.cloned.1.call-done) | copy-start | bytes 1179652
  282.3 9.2 %copy-start.25 = (bf16[768,768]{1,0:T(8,128)(2,1)S(1)}, bf16[768,768]{1,0:T(8,128)(2,1)}, u32[]{:S(2)}) copy-start(bf16[768,768]{1,0:T(8,128)(2,1)} %all-gather.13.cloned.1.call-done) | copy-start | bytes 3538948
  291.6 45.7 %copy-start.68 = (f32[256]{0:T(256)S(1)}, f32[256]{0:T(256)}, u32[]{:S(2)}) copy-start(f32[256]{0:T(256)} %get-tuple-element.74) | copy-start | bytes 3076
  (39 other events, 106.1 us)
Sparse Core Ops, SparseCore 0:
  9.6 11.9 all-gather.12
  23.1 10.3 all-gather.10
  35.1 10.3 all-gather.8
  46.9 10.4 all-gather.14
  96.4 9.1 all-gather.16
  126.1 7.5 all-gather.18
  147.6 10.2 reduce-scatter.6
  160.2 10.2 reduce-scatter.4
  224.4 7.5 reduce-scatter.10
  236.2 7.9 reduce-scatter.8
  250.4 193.2 all-reduce.3
where the time goes:
time: 464 us; the launch traced here: 456 us
  waiting for transfers between devices  162 us (35%)
  matrix products  108 us (23%)
  blocking collectives  79.8 us (17%)
  local copies, waits for them, and re-layouts  44 us (9%)
  other arithmetic  25.3 us (5%)
  starting transfers between devices  21.5 us (5%)
  between operations  15.1 us (3%)
    psum x1, waiting for transfers between devices, on_device(): lax.psum((grad_w_query, grad_w_key, grad_w_value, grad_w_output, grad_rou...  105 us
    psum x1, blocking collectives, on_device(): lax.psum((grad_w_query, grad_w_key, grad_w_value, grad_w_output, grad_rou...  41.7 us
    all_to_all x1, blocking collectives, on_device(): lax.all_to_all(grad_send.reshape(experts, capacity, model_width), 'expert...  25.3 us
    dot_general x2, matrix products, attend_backward(): jnp.einsum('hrk,rkb->hb', grad_scores, bucket_hot, precision=highest)  18 us
    all_to_all x1, waiting for transfers between devices, on_device(): lax.all_to_all(expert_result.astype(jnp.bfloat16), 'expert', split_axis=0...  15.1 us
    all_to_all x1, waiting for transfers between devices, on_device(): lax.all_to_all(send_rows.reshape(experts, capacity, model_width), 'expert...  14.7 us
    all_to_all x1, waiting for transfers between devices, on_device(): lax.all_to_all(grad_rows_in.astype(jnp.bfloat16), 'expert', split_axis=0,...  14.3 us
    mul x2, local copies, waits for them, and re-layouts, attend_backward(): grad_scores = probabilities * (grad_probs - row_dot)  10.4 us
  transfers between devices with their start and end apart: 14, of which 7 were waited for; matrix products, arithmetic and copies ran while one was open for 28% of the time, Pallas kernels for 0%

commit v1 on v0

v1 whole, which is shorter than its diff:
```python
import functools

import jax
import jax.numpy as jnp
from jax import lax
from jax.experimental import pallas as pl
from jax.experimental.pallas import tpu as pltpu
from jax.sharding import PartitionSpec as P

bucket_edges = (8, 12, 16, 23, 32, 46, 64, 91)
epsilon = 1e-06
score_scale = 0.125
masked_score = -1e30
highest = lax.Precision.HIGHEST
contract_last = (((1,), (1,)), ((), ()))
contract_first = (((0,), (0,)), ((), ()))


def bucket_of(offsets):
    distance = jnp.abs(offsets)
    far_bucket = 8 + sum(
        ((distance >= boundary).astype(jnp.int32) for boundary in bucket_edges[1:])
    )
    near_bucket = jnp.where(distance < 8, distance, far_bucket)
    return near_bucket + 16 * (offsets > 0).astype(jnp.int32)


def rms_forward(hidden, gain_value):
    scale = lax.rsqrt(jnp.mean(hidden * hidden, axis=-1, keepdims=True) + epsilon)
    return (hidden * scale * gain_value, scale)


def rms_backward(hidden, scale, gain_value, grad_normed):
    weighted = grad_normed * gain_value
    grad_gain = jnp.sum(grad_normed * hidden * scale, axis=0)
    grad_hidden = scale * weighted - hidden * (scale * scale * scale) * jnp.mean(
        weighted * hidden, axis=-1, keepdims=True
    )
    return (grad_hidden, grad_gain)


def toeplitz(seed_rows, row_count):
    rows = seed_rows
    while rows.shape[0] < row_count:
        rows = jnp.concatenate([rows, pltpu.roll(rows, rows.shape[0], 1)], axis=0)
    return rows


def fold_rows(block, width):
    row_count, columns = block.shape
    rows = jnp.concatenate([block, jnp.zeros((row_count, width - columns), block.dtype)], axis=1)
    while rows.shape[0] > 8:
        half = rows.shape[0] // 2
        rows = rows[:half] + pltpu.roll(rows[half:], width - half, 1)
    return rows


def attend_kernel(head_size, q_ref, k_ref, v_ref, seed_ref, qdoc_ref, kdoc_ref, o_ref, p_ref):
    row_count, key_count = q_ref.shape[0], k_ref.shape[0]
    same_doc = qdoc_ref[...] == kdoc_ref[...]
    outs = []
    for h in range(seed_ref.shape[0]):
        cols = slice(h * head_size, (h + 1) * head_size)
        bias = toeplitz(seed_ref[h], row_count)[:, :key_count]
        scores = (
            lax.dot_general(
                q_ref[:, cols], k_ref[:, cols], contract_last, preferred_element_type=jnp.float32
            )
            * score_scale
            + bias
        )
        scores = jnp.where(same_doc, scores, masked_score)
        weights = jnp.exp(scores - jnp.max(scores, axis=-1, keepdims=True))
        probs = weights / jnp.sum(weights, axis=-1, keepdims=True)
        p_ref[h] = probs
        outs.append(
            jnp.dot(probs.astype(jnp.bfloat16), v_ref[:, cols], preferred_element_type=jnp.float32)
        )
    o_ref[...] = jnp.concatenate(outs, axis=1).astype(o_ref.dtype)


def attend_back_kernel(
    head_size, width, q_ref, k_ref, v_ref, p_ref, do_ref, dq_ref, dk_ref, dv_ref, fold_ref
):
    dqs, dks, dvs = [], [], []
    for h in range(p_ref.shape[0]):
        cols = slice(h * head_size, (h + 1) * head_size)
        probs, grad_out = p_ref[h], do_ref[:, cols]
        grad_probs = lax.dot_general(
            grad_out, v_ref[:, cols], contract_last, preferred_element_type=jnp.float32
        )
        row_dot = jnp.sum(probs * grad_probs, axis=-1, keepdims=True)
        grad_scores = probs * (grad_probs - row_dot)
        fold_ref[h] = fold_rows(grad_scores, width)
        grad_low = grad_scores.astype(jnp.bfloat16)
        dqs.append(
            jnp.dot(grad_low, k_ref[:, cols], preferred_element_type=jnp.float32) * score_scale
        )
        dks.append(
            lax.dot_general(
                grad_low, q_ref[:, cols], contract_first, preferred_element_type=jnp.float32
            )
            * score_scale
        )
        dvs.append(
            lax.dot_general(
                probs.astype(jnp.bfloat16),
                grad_out,
                contract_first,
                preferred_element_type=jnp.float32,
            )
        )
    dq_ref[...] = jnp.concatenate(dqs, axis=1).astype(dq_ref.dtype)
    dk_ref[...] = jnp.concatenate(dks, axis=1).astype(dk_ref.dtype)
    dv_ref[...] = jnp.concatenate(dvs, axis=1).astype(dv_ref.dtype)


def attend_forward(queries, keys_values, seed_rows, query_docs, key_docs, head_size):
    rows, width = queries.shape
    keys = keys_values.shape[0]
    heads, _, lanes = seed_rows.shape
    pair = 128 // head_size
    steps = heads // pair
    return pl.pallas_call(
        functools.partial(attend_kernel, head_size),
        grid=(steps,),
        in_specs=[
            pl.BlockSpec((rows, 128), lambda i: (0, i)),
            pl.BlockSpec((keys, 128), lambda i: (0, i)),
            pl.BlockSpec((keys, 128), lambda i: (0, i + steps)),
            pl.BlockSpec((pair, 8, lanes), lambda i: (i, 0, 0)),
            pl.BlockSpec((rows, 1), lambda i: (0, 0)),
            pl.BlockSpec((1, keys), lambda i: (0, 0)),
        ],
        out_specs=[
            pl.BlockSpec((rows, 128), lambda i: (0, i)),
            pl.BlockSpec((pair, rows, keys), lambda i: (i, 0, 0)),
        ],
        out_shape=[
            jax.ShapeDtypeStruct((rows, width), jnp.bfloat16),
            jax.ShapeDtypeStruct((heads, rows, keys), jnp.float32),
        ],
        compiler_params=pltpu.CompilerParams(vmem_limit_bytes=40 << 20),
        cost_estimate=pl.CostEstimate(
            flops=4 * rows * keys * width, bytes_accessed=8 << 20, transcendentals=0
        ),
        name="attend_forward",
    )(queries, keys_values, keys_values, seed_rows, query_docs[:, None], key_docs[None, :])


def attend_backward(queries, keys_values, probs, grad_attn, head_size, lanes):
    rows, width = queries.shape
    keys = keys_values.shape[0]
    heads = probs.shape[0]
    pair = 128 // head_size
    steps = heads // pair
    row_spec = pl.BlockSpec((rows, 128), lambda i: (0, i))
    key_spec = pl.BlockSpec((keys, 128), lambda i: (0, i))
    return pl.pallas_call(
        functools.partial(attend_back_kernel, head_size, lanes),
        grid=(steps,),
        in_specs=[
            row_spec,
            key_spec,
            pl.BlockSpec((keys, 128), lambda i: (0, i + steps)),
            pl.BlockSpec((pair, rows, keys), lambda i: (i, 0, 0)),
            row_spec,
        ],
        out_specs=[
            row_spec,
            key_spec,
            key_spec,
            pl.BlockSpec((pair, 8, lanes), lambda i: (i, 0, 0)),
        ],
        out_shape=[
            jax.ShapeDtypeStruct((rows, width), jnp.bfloat16),
            jax.ShapeDtypeStruct((keys, width), jnp.bfloat16),
            jax.ShapeDtypeStruct((keys, width), jnp.bfloat16),
            jax.ShapeDtypeStruct((heads, 8, lanes), jnp.float32),
        ],
        compiler_params=pltpu.CompilerParams(vmem_limit_bytes=40 << 20),
        cost_estimate=pl.CostEstimate(
            flops=8 * rows * keys * width, bytes_accessed=9 << 20, transcendentals=0
        ),
        name="attend_backward",
    )(queries, keys_values, keys_values, probs, grad_attn)


def on_device(
    tokens,
    out_grad,
    seq_lengths,
    expert_ids,
    w_query,
    w_key,
    w_value,
    w_output,
    w_router,
    gain_attn,
    gain_ffn,
    bias_table,
    expert_in,
    expert_out,
):
    tok_count, width = tokens.shape
    half_width = w_query.shape[0]
    experts = w_router.shape[1]
    capacity = 2 * tok_count // experts
    half_buckets, heads = bias_table.shape
    buckets = 2 * half_buckets
    inner = w_query.shape[1]
    head_size = inner // heads
    shard_count = lax.axis_size("shard")
    shard_index = lax.axis_index("shard")
    key_count = shard_count * tok_count
    low, f32 = jnp.bfloat16, jnp.float32

    def dot(a, b):
        return jnp.dot(a, b, preferred_element_type=f32)

    def dot_tn(a, b):
        return lax.dot_general(a, b, contract_first, preferred_element_type=f32)

    def dot_nt(a, b):
        return lax.dot_general(a, b, contract_last, preferred_element_type=f32)

    def column(flat):
        flat = flat.reshape(-1)
        return jnp.pad(flat, (0, half_width - flat.shape[0]))[:, None]

    small = jnp.concatenate([w_router, gain_attn[:, None], gain_ffn[:, None], column(bias_table)], 1)
    small = lax.all_gather(small, "shard", axis=0, tiled=True)
    qkv_weight = lax.all_gather(
        jnp.concatenate([w_query, w_key, w_value], axis=1), "shard", axis=0, tiled=True
    )
    output_weight = lax.all_gather(w_output, "shard", axis=0, tiled=True)
    router_float = small[:, :experts].astype(f32)
    gain_one = small[:, experts].astype(f32)
    gain_two = small[:, experts + 1].astype(f32)
    table = (
        small[:, experts + 2]
        .reshape(shard_count, half_width)[:, : half_buckets * heads]
        .reshape(buckets, heads)
        .astype(f32)
    )
    x_float = tokens.astype(f32)
    normed_one, scale_one = rms_forward(x_float, gain_one)
    normed_low = normed_one.astype(low)
    kv_local = dot(normed_low, qkv_weight[:, inner:]).astype(low)
    keys_values = lax.all_gather(kv_local, "shard", axis=0, tiled=True)
    queries = dot(normed_low, qkv_weight[:, :inner]).astype(low)

    lanes = key_count + tok_count
    lane = jnp.arange(lanes, dtype=jnp.int32)
    offsets = jnp.where(lane < key_count, lane, lane - lanes) - shard_index * tok_count
    bucket_hot = (
        bucket_of(offsets)[:, None] == jnp.arange(buckets, dtype=jnp.int32)[None, :]
    ).astype(f32)
    offset_bias = jnp.einsum("lb,bh->hl", bucket_hot, table, precision=highest)
    seed_rows = jnp.stack([jnp.roll(offset_bias, r, axis=1) for r in range(8)], axis=1)

    seq_ends = jnp.cumsum(seq_lengths[0])[:-1]
    key_places = jnp.arange(key_count, dtype=jnp.int32)
    key_docs = jnp.sum((key_places[:, None] >= seq_ends[None, :]).astype(jnp.int32), axis=1)
    query_docs = lax.dynamic_slice_in_dim(key_docs, shard_index * tok_count, tok_count, 0)
    attn_part, probs = attend_forward(
        queries, keys_values, seed_rows, query_docs, key_docs, head_size
    )
    hidden_one = x_float + dot(attn_part, output_weight)
    normed_two, scale_two = rms_forward(hidden_one, gain_two)
    logits = jnp.dot(normed_two, router_float, precision=highest)
    route_probs = jax.nn.softmax(logits, axis=-1)
    route_flat = expert_ids[:, 0]
    expert_range = jnp.arange(experts, dtype=jnp.int32)
    route_int = (route_flat[:, None] == expert_range[None, :]).astype(jnp.int32)
    route_hot = route_int.astype(f32)
    gate_value = jnp.sum(route_probs * route_hot, axis=1)
    tok_range = jnp.arange(tok_count, dtype=jnp.int32)
    earlier = (tok_range[:, None] >= tok_range[None, :]).astype(low)
    counts = dot(earlier, route_hot.astype(low))
    slot_ranks = jnp.sum(counts * route_hot, axis=1).astype(jnp.int32) - 1
    slot_ids = route_flat * capacity + slot_ranks
    slot_hot = (
        slot_ids[:, None] == jnp.arange(experts * capacity, dtype=jnp.int32)[None, :]
    ).astype(low)

    def dispatch(rows):
        sent = dot_tn(slot_hot, rows).astype(low).reshape(experts, capacity, width)
        got = lax.all_to_all(sent, "expert", split_axis=0, concat_axis=0, tiled=True)
        return lax.all_gather(got, "shard", axis=0, tiled=True).reshape(-1, width)

    def collect(rows):
        halves = lax.psum_scatter(
            rows.reshape(shard_count * experts, capacity, width).astype(low),
            "shard",
            scatter_dimension=0,
            tiled=True,
        )
        got = lax.all_to_all(halves, "expert", split_axis=0, concat_axis=0, tiled=True)
        return dot(slot_hot, got.reshape(-1, width))

    grad_out = out_grad.astype(f32)
    expert_rows = dispatch(normed_two.astype(low))
    grad_rows = dispatch((gate_value[:, None] * grad_out).astype(low))
    weight_in = expert_in[0]
    weight_out = expert_out[0]
    pre_act = dot(expert_rows, weight_in)
    act_low = jax.nn.gelu(pre_act).astype(low)
    result_float = collect(dot(act_low, weight_out))
    grad_act = dot_nt(grad_rows, weight_out)
    _, gelu_pull = jax.vjp(jax.nn.gelu, pre_act)
    grad_pre = gelu_pull(grad_act)[0].astype(low)
    grad_expert_tok = collect(dot_nt(grad_pre, weight_in))

    layer_out = (hidden_one + gate_value[:, None] * result_float).astype(low)
    grad_gate = jnp.sum(grad_out * result_float, axis=1)
    grad_logits = gate_value[:, None] * (route_hot - route_probs) * grad_gate[:, None]
    grad_router = jnp.einsum("td,te->de", normed_two, grad_logits, precision=highest)
    grad_normed_two = (
        jnp.einsum("te,de->td", grad_logits, router_float, precision=highest) + grad_expert_tok
    )
    grad_hidden_norm, grad_gain_two = rms_backward(hidden_one, scale_two, gain_two, grad_normed_two)
    grad_hidden = grad_out + grad_hidden_norm
    grad_branch = grad_hidden.astype(low)

    def whole_sum(parts):
        packed = jnp.concatenate([part.astype(low) for part in parts], axis=1)
        extra = -packed.shape[1] % 128
        packed = jnp.pad(packed, ((0, 0), (0, extra)))
        halves = lax.psum_scatter(packed, "shard", scatter_dimension=0, tiled=True)
        return lax.psum(halves, "expert").astype(f32)

    first_sum = whole_sum([dot_tn(attn_part, grad_branch), grad_router, grad_gain_two[:, None]])
    grad_attn = dot_nt(grad_branch, output_weight).astype(low)
    grad_queries, grad_k_part, grad_v_part, folded = attend_backward(
        queries, keys_values, probs, grad_attn, head_size, lanes
    )
    grad_kv = lax.psum_scatter(
        jnp.concatenate([grad_k_part, grad_v_part], axis=1),
        "shard",
        scatter_dimension=0,
        tiled=True,
    )
    offset_sums = sum(jnp.roll(folded[:, r], -r, axis=1) for r in range(8))
    grad_table = jnp.einsum("hl,lb->bh", offset_sums, bucket_hot, precision=highest)
    table_column = jnp.pad(
        grad_table.reshape(shard_count, half_buckets * heads),
        ((0, 0), (0, half_width - half_buckets * heads)),
    ).reshape(-1, 1)
    grad_qkv = jnp.concatenate([grad_queries, grad_kv], axis=1)
    grad_normed_one = dot_nt(grad_qkv, qkv_weight)
    grad_x_norm, grad_gain_one = rms_backward(x_float, scale_one, gain_one, grad_normed_one)
    grad_tokens = grad_hidden + grad_x_norm
    second_sum = whole_sum([dot_tn(normed_low, grad_qkv), grad_gain_one[:, None], table_column])
    grad_w_out = dot_tn(act_low, grad_rows)
    grad_w_in = dot_tn(expert_rows, grad_pre)
    return (
        layer_out,
        grad_tokens,
        second_sum[:, :inner],
        second_sum[:, inner : 2 * inner],
        second_sum[:, 2 * inner : 3 * inner],
        first_sum[:, :width],
        first_sum[:, width : width + experts],
        second_sum[:, 3 * inner],
        first_sum[:, width + experts],
        second_sum[: half_buckets * heads, 3 * inner + 1].reshape(half_buckets, heads),
        grad_w_in[None],
        grad_w_out[None],
    )


def solution(mesh):
    placed = (
        P(("expert", "shard"), None),
        P(("expert", "shard"), None),
        P("expert", None),
        P(("expert", "shard"), None),
        P("shard", None),
        P("shard", None),
        P("shard", None),
        P("shard", None),
        P("shard", None),
        P("shard"),
        P("shard"),
        P("shard", None),
        P("expert", None, "shard"),
        P("expert", "shard", None),
    )
    return jax.shard_map(
        on_device,
        mesh=mesh,
        in_specs=placed,
        out_specs=(
            P(("expert", "shard"), None),
            P(("expert", "shard"), None),
            P("shard", None),
            P("shard", None),
            P("shard", None),
            P("shard", None),
            P("shard", None),
            P("shard"),
            P("shard"),
            P("shard", None),
            P("expert", None, "shard"),
            P("expert", "shard", None),
        ),
        check_vma=False,
    )
```

time: 464 us -> 409 us (0.88); the launches traced: 456 us -> 407 us
  blocking collectives: 79.8 us -> 27.3 us
  waiting for transfers between devices: 162 us -> 210 us
  matrix products: 108 us -> 64.1 us
  Pallas kernels: 0 us -> 21 us
  other arithmetic: 25.3 us -> 13.8 us
  starting transfers between devices: 21.5 us -> 16.6 us
  local copies, waits for them, and re-layouts: 44 us -> 39.2 us
    dot_general x34 -> x20, matrix products: 103 us -> 59.2 us  [the longest x8 23.3 us: dot(): return jnp.dot(a, b, preferred_element_type=f32)]
    psum x1 -> x0, blocking collectives: 41.7 us -> none  [on_device(): lax.psum((grad_w_query, grad_w_key, grad_w_value, grad_w_output, grad_rou...]
    psum x1, waiting for transfers between devices: 105 us -> 131 us  [whole_sum(): return lax.psum(halves, 'expert').astype(f32)]
    pallas_call x0 -> x2, Pallas kernels: none -> 21 us  [the longest x1 11.6 us: attend_forward(): pl.pallas_call(functools.partial(attend_kernel, head_size), grid=(steps,)...]
    all_gather x6 -> x5, waiting for transfers between devices: 0.42 us -> 17.4 us  [the longest x1 12.6 us: on_device(): lax.all_gather(jnp.concatenate([w_query, w_key, w_value], axis=1), 'shard...]
    all_gather x6 -> x1, blocking collectives: 12.7 us -> 1.95 us  [on_device(): small = lax.all_gather(small, 'shard', axis=0, tiled=True)]
    mul x2 -> x0, local copies, waits for them, and re-layouts: 10.4 us -> none  [attend_backward(): grad_scores = probabilities * (grad_probs - row_dot)]
    dot_general x2 -> x0, local copies, waits for them, and re-layouts: 9.85 us -> none  [score_block(): jnp.einsum('rkb,hb->hrk', bucket_hot, table_part, precision=highest)]
  transfers between devices with their start and end apart: 14 -> 14, of which waited for: 7 -> 9; matrix products, arithmetic and copies ran while one was open for 28% -> 19% of each run, Pallas kernels for 0% -> 3%
where the time goes in v1:
time: 409 us; the launch traced here: 407 us
  waiting for transfers between devices  210 us (51%)
  matrix products  64.1 us (16%)
  local copies, waits for them, and re-layouts  39.2 us (10%)
  blocking collectives  27.3 us (7%)
  Pallas kernels  21 us (5%)
  starting transfers between devices  16.6 us (4%)
  between operations  14.9 us (4%)
  other arithmetic  13.8 us (3%)
    psum x1, waiting for transfers between devices, whole_sum(): return lax.psum(halves, 'expert').astype(f32)  131 us
    all_to_all x2, waiting for transfers between devices, collect(): lax.all_to_all(halves, 'expert', split_axis=0, concat_axis=0, tiled=True)  30.1 us
    all_to_all x1, blocking collectives, dispatch(): lax.all_to_all(sent, 'expert', split_axis=0, concat_axis=0, tiled=True)  25.3 us
    dot_general x8, matrix products, dot(): return jnp.dot(a, b, preferred_element_type=f32)  23.3 us
    dot_general x6, matrix products, dot_tn(): return lax.dot_general(a, b, contract_first, preferred_element_type=f32)  18.2 us
    dot_general x4, matrix products, dot_nt(): return lax.dot_general(a, b, contract_last, preferred_element_type=f32)  17.1 us
    all_to_all x1, waiting for transfers between devices, dispatch(): lax.all_to_all(sent, 'expert', split_axis=0, concat_axis=0, tiled=True)  15.9 us
    unnamed x122, local copies, waits for them, and re-layouts  15.8 us
  transfers between devices with their start and end apart: 14, of which 9 were waited for; matrix products, arithmetic and copies ran while one was open for 19% of the time, Pallas kernels for 3%

profile of v1, /device:TPU:0, one launch (start us, length us, event | category | flops | bytes accessed | tf_op | source)
XLA Modules:
  0.0 407.1 jit_solution(13949438219763334067)
XLA Ops:
  7.3 2.9 pad_maximum_fusion
  10.5 1.9 all_gather.18
  13.2 12.6 %all-gather.6.cloned.1.call-done = bf16[768,2304]{1,0:T(8,128)(2,1)} async-done(((bf16[384,2304]{1,0:T(8,128)(2,1)}), bf16[768,2304]{1,0:T(8,128)(2,1)}) %all-gather.6.cloned.1.call-update) | async-done | bytes 3538960 | tf_op jit(solution)/shard_map/all_gather | solution.py:233
  25.8 3.4 convolution_convert_fusion.1
  33.8 1.8 convolution_convert_fusion.6.q_ref
  35.5 4.8 %all-gather.8.cloned.1.call-done.k_ref.v_ref = bf16[512,1536]{1,0:T(8,128)(2,1)} async-done(((bf16[256,1536]{1,0:T(8,128)(2,1)}), bf16[512,1536]{1,0:T(8,128)(2,1)}) %all-gather.8.cloned.1.call-update) | async-done | bytes 1572880 | tf_op jit(solution)/shard_map/all_gather | solution.py:250
  40.4 1.4 copy-done.2
  42.7 11.6 %attend_forward.1 = (bf16[256,768]{1,0:T(8,128)(2,1)S(1)}, f32[12,256,512]{2,1,0:T(8,128)S(1)}) custom-call(bf16[256,768]{1,0:T(8,128)(2,1)S(1)} %convolution_convert_fusion.6.q_ref, bf16[512,1536]{1,0:T(8,128)(2,1)S(1)} %copy-done.2, bf16[512,1536]{1,0:T(8,128)(2,1)S(1)} %copy-done.2, f32[12,8,768]{2,1,0:T(8,128)S(1)} %stack.35.seed_ref, ...), custom_call_target="tpu_custom_call" | custom-call | flops 402653184 | bytes 8388608 | tf_op jit(solution)/shard_map/attend_forward/pallas_call | solution.py:124
  54.3 2.6 copy-done.4
  57.0 2.7 multiply_reduce_fusion.2
  60.3 2.6 convolution_convert_fusion.4
  62.9 6.8 %all-to-all-start = ((bf16[16,32,768]{2,1,0:T(8,128)(2,1)}), bf16[16,32,768]{2,1,0:T(8,128)(2,1)}, u32[]{:S(2)}, u32[]{:S(2)}) async-start(bf16[16,32,768]{2,1,0:T(8,128)(2,1)} %bitcast.113), calls=%async_computation | async-start | bytes 1572864 | tf_op jit(solution)/shard_map/all_to_all | solution.py:289
  69.8 1.8 fusion.119
  73.9 15.9 %all-to-all-done = bf16[16,32,768]{2,1,0:T(8,128)(2,1)} async-done(((bf16[16,32,768]{2,1,0:T(8,128)(2,1)}), bf16[16,32,768]{2,1,0:T(8,128)(2,1)}, u32[]{:S(2)}, u32[]{:S(2)}) %all-to-all-start) | async-done | bytes 786464 | tf_op jit(solution)/shard_map/all_to_all | solution.py:289
  89.9 1.3 convolution_convert_fusion.3
  91.2 25.3 %all_to_all.20 = bf16[16,32,768]{2,1,0:T(8,128)(2,1)} all-to-all(bf16[16,32,768]{2,1,0:T(8,128)(2,1)S(1)} %bitcast.114), channel_id=1, replica_groups=mesh['expert'=16,'shard'=2] {'expert'}, dimensions={0} | all-to-all | bytes 1572864 | tf_op jit(solution)/shard_map/all_to_all | solution.py:289
  116.7 6.7 %multiply_convert_fusion = (bf16[1024,1536]{1,0:T(8,128)(2,1)S(1)}, f32[1024,1536]{1,0:T(8,128)}) fusion(bf16[1024,768]{1,0:T(8,128)(2,1)} %bitcast.116, bf16[1,768,1536]{2,1,0:T(8,128)(2,1)S(1)} %copy-done), kind=kOutput, calls=%fused_computation.9 | convolution fusion | flops 2430074880 | bytes 13369344 | tf_op jit(solution)/shard_map/dot_general | solution.py:219
  123.4 1.7 copy-done.54
  125.1 3.7 fusion.18
  129.0 8.4 %fusion.6 = bf16[1024,1536]{1,0:T(8,128)(2,1)S(1)} fusion(f32[1024,1536]{1,0:T(8,128)} %get-tuple-element.98, bf16[1024,768]{1,0:T(8,128)(2,1)} %bitcast.132, bf16[1,1536,768]{2,1,0:T(8,128)(2,1)} %param.27), kind=kOutput, calls=%fused_computation.8 | convolution fusion | flops 2447376384 | bytes 13369344 | tf_op jit(solution)/shard_map/dot_general | solution.py:225
  137.4 1.7 copy-done.18
  139.1 3.7 fusion.21
  143.0 4.3 %all-to-all-start.1 = ((bf16[16,32,768]{2,1,0:T(8,128)(2,1)}), bf16[16,32,768]{2,1,0:T(8,128)(2,1)}, u32[]{:S(2)}, u32[]{:S(2)}) async-start(bf16[16,32,768]{2,1,0:T(8,128)(2,1)} %reduce-scatter.8.cloned.1.call-done), calls=%async_computation.2 | async-start | bytes 1572864 | tf_op jit(solution)/shard_map/all_to_all | solution.py:299
  147.3 3.1 reduce-scatter.10.cloned.1.call-done
  150.4 15.4 %all-to-all-done.1 = bf16[16,32,768]{2,1,0:T(8,128)(2,1)} async-done(((bf16[16,32,768]{2,1,0:T(8,128)(2,1)}), bf16[16,32,768]{2,1,0:T(8,128)(2,1)}, u32[]{:S(2)}, u32[]{:S(2)}) %all-to-all-start.1) | async-done | bytes 786464 | tf_op jit(solution)/shard_map/all_to_all | solution.py:299
  165.8 4.6 %all-to-all-start.3 = ((bf16[16,32,768]{2,1,0:T(8,128)(2,1)}), bf16[16,32,768]{2,1,0:T(8,128)(2,1)}, u32[]{:S(2)}, u32[]{:S(2)}) async-start(bf16[16,32,768]{2,1,0:T(8,128)(2,1)} %reduce-scatter.10.cloned.1.call-done), calls=%async_computation.5 | async-start | bytes 1572864 | tf_op jit(solution)/shard_map/all_to_all | solution.py:299
  170.5 2.4 fusion.26
  173.0 1.4 fusion.87
  174.4 14.7 %all-to-all-done.3 = bf16[16,32,768]{2,1,0:T(8,128)(2,1)} async-done(((bf16[16,32,768]{2,1,0:T(8,128)(2,1)}), bf16[16,32,768]{2,1,0:T(8,128)(2,1)}, u32[]{:S(2)}, u32[]{:S(2)}) %all-to-all-start.3) | async-done | bytes 786464 | tf_op jit(solution)/shard_map/all_to_all | solution.py:299
  189.1 2.3 multiply_reduce_fusion
  191.4 2.3 convert_add_fusion.1
  194.3 9.3 %attend_backward.1 = (bf16[256,768]{1,0:T(8,128)(2,1)S(1)}, bf16[512,768]{1,0:T(8,128)(2,1)S(1)}, bf16[512,768]{1,0:T(8,128)(2,1)S(1)}, f32[12,8,768]{2,1,0:T(8,128)S(1)}) custom-call(bf16[256,768]{1,0:T(8,128)(2,1)S(1)} %convolution_convert_fusion.6.q_ref, bf16[512,1536]{1,0:T(8,128)(2,1)S(1)} %copy-done.3, bf16[512,1536]{1,0:T(8,128)(2,1)S(1)} %copy-done.3, ...), custom_call_target="tpu_custom_call" | custom-call | flops 805306368 | bytes 9437184 | tf_op jit(solution)/shard_map/attend_backward/pallas_call | solution.py:159
  205.7 1.8 convolution_convert_fusion.7
  212.8 1.3 reduce-scatter.12.cloned.1.call-done
  215.4 4.5 %fusion.36 = (bf16[768]{0:T(1024)(128)(2,1)S(1)}, f32[256]{0:T(256)S(1)}, f32[256,768]{1,0:T(8,128)}) fusion(bf16[256,768]{1,0:T(8,128)(2,1)S(1)} %copy-done.13, f32[256]{0:T(256)S(1)} %copy-done.38, f32[768]{0:T(1024)S(1)} %copy-done.27, bf16[256,2304]{1,0:T(8,128)(2,1)S(1)} %constant_dynamic-update-slice_fusion, ...), kind=kOutput, calls=%fused_computation.58 | convolution fusion | flops 907344896 | bytes 5904896 | tf_op jit(solution)/shard_map/dot_general | solution.py:225
  220.7 2.5 convolution_convert_fusion
  223.2 5.3 %concatenate.92 = bf16[768,2306]{1,0:T(8,128)(2,1)} concatenate(bf16[768,2304]{1,0:T(8,128)(2,1)S(1)} %convolution_convert_fusion, bf16[768,1]{1,0:T(8,128)(2,1)} %convert_element_type.253, bf16[768,1]{1,0:T(8,128)(2,1)} %bitcast.118), dimensions={1} | concatenate | bytes 7084032 | tf_op jit(solution)/shard_map/concatenate | solution.py:327
  228.5 4.2 %pad.19 = bf16[768,2432]{1,0:T(8,128)(2,1)} pad(bf16[768,2306]{1,0:T(8,128)(2,1)} %concatenate.92, bf16[]{:T(256)} %constant.28.clone.1), padding=0_0x0_126 | pad | bytes 7277570 | tf_op jit(solution)/shard_map/jit(_pad)/pad | solution.py:329
  232.8 2.3 copy.71
  235.1 10.6 %reduce-scatter.14.cloned.1.call-done = bf16[384,2432]{1,0:T(8,128)(2,1)} async-done(((bf16[768,2432]{1,0:T(8,128)(2,1)}), bf16[384,2432]{1,0:T(8,128)(2,1)}) %reduce-scatter.14.cloned.1.call-update) | async-done | bytes 1867792 | tf_op jit(solution)/shard_map/reduce_scatter | solution.py:330
  245.8 6.9 %convolution_bitcast_fusion = f32[1,1536,768]{2,1,0:T(8,128)} fusion(bf16[1024,1536]{1,0:T(8,128)(2,1)} %copy-done.54, bf16[1024,768]{1,0:T(8,128)(2,1)S(1)} %bitcast.133), kind=kOutput, calls=%fused_computation.11 | convolution fusion | flops 2415919104 | bytes 9437184 | tf_op jit(solution)/shard_map/dot_general | solution.py:222
  252.7 4.4 %convolution_bitcast_fusion.1 = f32[1,768,1536]{2,1,0:T(8,128)} fusion(bf16[1024,768]{1,0:T(8,128)(2,1)S(1)} %bitcast.117, bf16[1024,1536]{1,0:T(8,128)(2,1)S(1)} %copy-done.19), kind=kOutput, calls=%fused_computation.12 | convolution fusion | flops 2415919104 | bytes 9437184 | tf_op jit(solution)/shard_map/dot_general | solution.py:222
  258.2 131.0 %all-reduce.7.cloned.1.call-done = (bf16[384,2432]{1,0:T(8,128)(2,1)}, bf16[384,896]{0,1:T(8,128)(2,1)}) async-done(((bf16[384,2432]{1,0:T(8,128)(2,1)}, bf16[384,896]{0,1:T(8,128)(2,1)}), (bf16[384,2432]{1,0:T(8,128)(2,1)}, bf16[384,896]{0,1:T(8,128)(2,1)})) %all-reduce.7.cloned.1.call-update) | async-done | bytes 2555920 | tf_op jit(solution)/shard_map/psum | solution.py:331
  389.3 1.5 slice.283
  391.8 2.3 convert_element_type.250
  394.2 1.9 fusion.118
  397.2 1.4 copy.69
  398.6 1.3 slice_reduce_fusion.3
  (229 shorter events, 23.9 us)
Async XLA Ops:
  7.2 109.5 %copy-start = (bf16[1,768,1536]{2,1,0:T(8,128)(2,1)S(1)}, bf16[1,768,1536]{2,1,0:T(8,128)(2,1)}, u32[]{:S(2)}) copy-start(bf16[1,768,1536]{2,1,0:T(8,128)(2,1)} %param.26) | copy-start | bytes 7077892
  7.2 5.2 %copy-start.12 = (bf16[256,768]{1,0:T(8,128)(2,1)S(1)}, bf16[256,768]{1,0:T(8,128)(2,1)}, u32[]{:S(2)}) copy-start(bf16[256,768]{1,0:T(8,128)(2,1)} %param.14) | copy-start | bytes 1179652
  7.2 18.5 %all-gather.6.cloned.1.call-start = ((), (), s32[]{:S(2)}) async-start(), calls=%async_computation.9 | async-start | bytes 5308416 | tf_op jit(solution)/shard_map/all_gather | solution.py:233
  10.2 30.2 %all-gather.8.cloned.1.call-start = ((), (), s32[]{:S(2)}) async-start(), calls=%async_computation.10 | async-start | bytes 2359296 | tf_op jit(solution)/shard_map/all_gather | solution.py:250
  12.4 17.5 %copy-start.24 = (bf16[768,19]{0,1:T(8,128)(2,1)}, bf16[768,19]{0,1:T(8,128)(2,1)S(1)}, u32[]{:S(2)}) copy-start(bf16[768,19]{0,1:T(8,128)(2,1)S(1)} %all_gather.18) | copy-start | bytes 87556
  12.5 21.3 %copy-start.26 = (f32[768]{0:T(1024)}, f32[768]{0:T(1024)S(1)}, u32[]{:S(2)}) copy-start(f32[768]{0:T(1024)S(1)} %get-tuple-element.77) | copy-start | bytes 9220
  12.5 47.8 %copy-start.28 = (f32[768]{0:T(1024)}, f32[768]{0:T(1024)S(1)}, u32[]{:S(2)}) copy-start(f32[768]{0:T(1024)S(1)} %get-tuple-element.76) | copy-start | bytes 9220
  13.2 20.5 %copy-start.37 = (f32[256]{0:T(256)}, f32[256]{0:T(256)S(1)}, u32[]{:S(2)}) copy-start(f32[256]{0:T(256)S(1)} %get-tuple-element.92) | copy-start | bytes 3076
  25.8 5.2 %copy-start.53 = (s32[1,4]{1,0:T(1,128)S(1)}, s32[1,4]{1,0:T(1,128)}, u32[]{:S(2)}) copy-start(s32[1,4]{1,0:T(1,128)} %param.16) | copy-start | bytes 52
  29.2 27.8 %all-gather.10.cloned.1.call-start = ((), (), s32[]{:S(2)}) async-start(), calls=%async_computation.11 | async-start | bytes 1769472 | tf_op jit(solution)/shard_map/all_gather | solution.py:236
  33.7 26.5 %copy-start.32 = (s32[256,1]{0,1:T(1,128)}, s32[256,1]{0,1:T(1,128)S(1)}, u32[]{:S(2)}) copy-start(s32[256,1]{0,1:T(1,128)S(1)} %multiply_add_fusion) | copy-start | bytes 3076
  59.7 30.3 %copy-start.17 = (bf16[256,768]{1,0:T(8,128)(2,1)S(1)}, bf16[256,768]{1,0:T(8,128)(2,1)}, u32[]{:S(2)}) copy-start(bf16[256,768]{1,0:T(8,128)(2,1)} %param.15) | copy-start | bytes 1179652
  62.9 27.0 %all-to-all-start = ((bf16[16,32,768]{2,1,0:T(8,128)(2,1)}), bf16[16,32,768]{2,1,0:T(8,128)(2,1)}, u32[]{:S(2)}, u32[]{:S(2)}) async-start(bf16[16,32,768]{2,1,0:T(8,128)(2,1)} %bitcast.113), calls=%async_computation | async-start | bytes 1572864 | tf_op jit(solution)/shard_map/all_to_all | solution.py:289
  69.7 46.9 %all-gather.12.cloned.1.call-start = ((), (), s32[]{:S(2)}) async-start(), calls=%async_computation.12 | async-start | bytes 2359296 | tf_op jit(solution)/shard_map/all_gather | solution.py:290
  89.9 39.1 %all-gather.14.cloned.1.call-start = ((), (), s32[]{:S(2)}) async-start(), calls=%async_computation.14 | async-start | bytes 2359296 | tf_op jit(solution)/shard_map/all_gather | solution.py:290
  116.6 26.4 %reduce-scatter.8.cloned.1.call-start = ((), (), s32[]{:S(2)}) async-start(), calls=%async_computation.13 | async-start | bytes 2359296 | tf_op jit(solution)/shard_map/reduce_scatter | solution.py:293
  116.7 8.4 %copy-start.51 = (bf16[1,1536,768]{2,1,0:T(8,128)(2,1)S(1)}, bf16[1,1536,768]{2,1,0:T(8,128)(2,1)}, u32[]{:S(2)}) copy-start(bf16[1,1536,768]{2,1,0:T(8,128)(2,1)} %param.27) | copy-start | bytes 7077892
  128.8 21.6 %reduce-scatter.10.cloned.1.call-start = ((), (), s32[]{:S(2)}) async-start(), calls=%async_computation.15 | async-start | bytes 2359296 | tf_op jit(solution)/shard_map/reduce_scatter | solution.py:293
  142.9 27.6 %copy-start.33 = (s32[256,1]{0,1:T(1,128)S(1)}, s32[256,1]{0,1:T(1,128)}, u32[]{:S(2)}) copy-start(s32[256,1]{0,1:T(1,128)} %copy-done.32) | copy-start | bytes 3076
  142.9 30.0 %copy-start.25 = (bf16[768,19]{0,1:T(8,128)(2,1)S(1)}, bf16[768,19]{0,1:T(8,128)(2,1)}, u32[]{:S(2)}) copy-start(bf16[768,19]{0,1:T(8,128)(2,1)} %copy-done.24) | copy-start | bytes 87556
  142.9 30.0 %copy-start.35 = (f32[256]{0:T(256)S(1)}, f32[256]{0:T(256)}, u32[]{:S(2)}) copy-start(f32[256]{0:T(256)} %copy-done.34) | copy-start | bytes 3076
  142.9 30.0 %copy-start.36 = (f32[256]{0:T(256)S(1)}, f32[256]{0:T(256)}, u32[]{:S(2)}) copy-start(f32[256]{0:T(256)} %multiply_reduce_fusion.3) | copy-start | bytes 3076
  142.9 30.0 %copy-start.40 = (s32[256,1]{0,1:T(1,128)S(1)}, s32[256,1]{0,1:T(1,128)}, u32[]{:S(2)}) copy-start(s32[256,1]{0,1:T(1,128)} %param.17) | copy-start | bytes 3076
  142.9 30.0 %copy-start.42 = (f32[256]{0:T(256)S(1)}, f32[256]{0:T(256)}, u32[]{:S(2)}) copy-start(f32[256]{0:T(256)} %copy-done.41) | copy-start | bytes 3076
  143.0 22.8 %all-to-all-start.1 = ((bf16[16,32,768]{2,1,0:T(8,128)(2,1)}), bf16[16,32,768]{2,1,0:T(8,128)(2,1)}, u32[]{:S(2)}, u32[]{:S(2)}) async-start(bf16[16,32,768]{2,1,0:T(8,128)(2,1)} %reduce-scatter.8.cloned.1.call-done), calls=%async_computation.2 | async-start | bytes 1572864 | tf_op jit(solution)/shard_map/all_to_all | solution.py:299
  147.3 41.8 %copy-start.29 = (f32[768]{0:T(1024)S(1)}, f32[768]{0:T(1024)}, u32[]{:S(2)}) copy-start(f32[768]{0:T(1024)} %copy-done.28) | copy-start | bytes 9220
  147.3 41.8 %copy-start.31 = (f32[256]{0:T(256)S(1)}, f32[256]{0:T(256)}, u32[]{:S(2)}) copy-start(f32[256]{0:T(256)} %copy-done.30) | copy-start | bytes 3076
  165.8 28.5 %slice-start = ((s8[6291456]{0:T(1024)(128)(4,1)}), s8[2097152]{0:T(1024)(128)(4,1)S(1)}, s32[]{:S(2)}) async-start(s8[6291456]{0:T(1024)(128)(4,1)} %bitcast.103), calls=%async_computation.20 | async-start | bytes 4194304
  165.8 23.2 %all-to-all-start.3 = ((bf16[16,32,768]{2,1,0:T(8,128)(2,1)}), bf16[16,32,768]{2,1,0:T(8,128)(2,1)}, u32[]{:S(2)}, u32[]{:S(2)}) async-start(bf16[16,32,768]{2,1,0:T(8,128)(2,1)} %reduce-scatter.10.cloned.1.call-done), calls=%async_computation.5 | async-start | bytes 1572864 | tf_op jit(solution)/shard_map/all_to_all | solution.py:299
  170.4 43.8 %reduce-scatter.12.cloned.1.call-start = ((), (), s32[]{:S(2)}) async-start(), calls=%async_computation.16 | async-start | bytes 2359296 | tf_op jit(solution)/shard_map/reduce_scatter | solution.py:338
  172.9 18.5 %copy-start.48 = (f32[256]{0:T(256)S(1)}, f32[256]{0:T(256)}, u32[]{:S(2)}) copy-start(f32[256]{0:T(256)} %get-tuple-element.93) | copy-start | bytes 3076
  189.1 5.3 %slice-start.1 = ((s8[6291456]{0:T(1024)(128)(4,1)}), s8[4194304]{0:T(1024)(128)(4,1)S(1)}, s32[]{:S(2)}) async-start(s8[6291456]{0:T(1024)(128)(4,1)} %bitcast.103), calls=%async_computation.21 | async-start | bytes 8388608
  193.8 9.9 %copy-start.9 = (f32[256,768]{1,0:T(8,128)}, f32[256,768]{1,0:T(8,128)S(1)}, u32[]{:S(2)}) copy-start(f32[256,768]{1,0:T(8,128)S(1)} %get-tuple-element.83) | copy-start | bytes 2359300
  205.7 27.1 %reduce-scatter.16.cloned.1.call-start = ((), (), s32[]{:S(2)}) async-start(), calls=%async_computation.18 | async-start | bytes 2064384
  210.3 35.5 %reduce-scatter.14.cloned.1.call-start = ((), (), s32[]{:S(2)}) async-start(), calls=%async_computation.17 | async-start | bytes 5603328 | tf_op jit(solution)/shard_map/reduce_scatter | solution.py:330
  210.7 4.7 %copy-start.13 = (bf16[256,768]{1,0:T(8,128)(2,1)S(1)}, bf16[256,768]{1,0:T(8,128)(2,1)}, u32[]{:S(2)}) copy-start(bf16[256,768]{1,0:T(8,128)(2,1)} %param.14) | copy-start | bytes 1179652
  210.7 4.7 %copy-start.27 = (f32[768]{0:T(1024)S(1)}, f32[768]{0:T(1024)}, u32[]{:S(2)}) copy-start(f32[768]{0:T(1024)} %copy-done.26) | copy-start | bytes 9220
  210.7 4.7 %copy-start.38 = (f32[256]{0:T(256)S(1)}, f32[256]{0:T(256)}, u32[]{:S(2)}) copy-start(f32[256]{0:T(256)} %copy-done.37) | copy-start | bytes 3076
  215.4 4.5 %copy-start.21 = (bf16[256,2304]{1,0:T(8,128)(2,1)}, bf16[256,2304]{1,0:T(8,128)(2,1)S(1)}, u32[]{:S(2)}) copy-start(bf16[256,2304]{1,0:T(8,128)(2,1)S(1)} %constant_dynamic-update-slice_fusion) | copy-start | bytes 3538948
  215.4 5.3 %copy-start.14 = (bf16[256,768]{1,0:T(8,128)(2,1)S(1)}, bf16[256,768]{1,0:T(8,128)(2,1)}, u32[]{:S(2)}) copy-start(bf16[256,768]{1,0:T(8,128)(2,1)} %param.14) | copy-start | bytes 1179652
  232.7 13.0 %copy-start.52 = (bf16[32,32,768]{2,1,0:T(8,128)(2,1)S(1)}, bf16[32,32,768]{2,1,0:T(8,128)(2,1)}, u32[]{:S(2)}) copy-start(bf16[32,32,768]{2,1,0:T(8,128)(2,1)} %all-gather.14.cloned.1.call-done) | copy-start | bytes 4718596
  232.7 156.5 %all-reduce.7.cloned.1.call-start = ((), (), s32[]{:S(2)}) async-start(), calls=%async_computation.19 | async-start | bytes 5111808 | tf_op jit(solution)/shard_map/psum | solution.py:331
  245.7 6.9 %copy-start.19 = (bf16[1024,1536]{1,0:T(8,128)(2,1)S(1)}, bf16[1024,1536]{1,0:T(8,128)(2,1)}, u32[]{:S(2)}) copy-start(bf16[1024,1536]{1,0:T(8,128)(2,1)} %copy-done.18) | copy-start | bytes 9437188
  245.8 6.9 %copy-start.22 = (bf16[32,32,768]{2,1,0:T(8,128)(2,1)S(1)}, bf16[32,32,768]{2,1,0:T(8,128)(2,1)}, u32[]{:S(2)}) copy-start(bf16[32,32,768]{2,1,0:T(8,128)(2,1)} %all-gather.12.cloned.1.call-done) | copy-start | bytes 4718596
  252.7 4.4 %copy-start.11 = (f32[256,768]{1,0:T(8,128)S(1)}, f32[256,768]{1,0:T(8,128)}, u32[]{:S(2)}) copy-start(f32[256,768]{1,0:T(8,128)} %copy-done.9) | copy-start | bytes 2359300
  252.7 4.4 %copy-start.15 = (bf16[256,768]{1,0:T(8,128)(2,1)S(1)}, bf16[256,768]{1,0:T(8,128)(2,1)}, u32[]{:S(2)}) copy-start(bf16[256,768]{1,0:T(8,128)(2,1)} %param.14) | copy-start | bytes 1179652
  389.2 4.9 %copy-start.8 = (bf16[384,2432]{1,0:T(8,128)(2,1)S(1)}, bf16[384,2432]{1,0:T(8,128)(2,1)}, u32[]{:S(2)}) copy-start(bf16[384,2432]{1,0:T(8,128)(2,1)} %get-tuple-element.78) | copy-start | bytes 5603332
  396.0 4.5 %copy-start.1 = (bf16[1,768,1536]{2,1,0:T(8,128)(2,1)S(1)}, bf16[1,768,1536]{2,1,0:T(8,128)(2,1)}, u32[]{:S(2)}) copy-start(bf16[1,768,1536]{2,1,0:T(8,128)(2,1)} %param.26) | copy-start | bytes 7077892
  (23 other events, 52.6 us)
Sparse Core Ops, SparseCore 0:
  10.3 15.3 all-gather.5
  29.3 11.0 all-gather.7
  41.9 10.3 all-gather.9
  90.0 9.2 all-gather.11
  116.7 7.5 all-gather.13
  128.9 8.2 reduce-scatter.7
  143.0 7.3 reduce-scatter.9
  205.8 8.3 reduce-scatter.11
  216.5 10.0 reduce-scatter.15
  232.8 12.8 reduce-scatter.13
  252.9 136.3 all-reduce.6

commit v2 on v1

--- a/solution.py
+++ b/solution.py
@@ -12,6 +12,7 @@
 score_scale = 0.125
 masked_score = -1e30
 highest = lax.Precision.HIGHEST
+MESH = pl.DeviceIdType.MESH
 contract_last = (((1,), (1,)), ((), ()))
 contract_first = (((0,), (0,)), ((), ()))
 
@@ -184,6 +185,146 @@
         ),
         name="attend_backward",
     )(queries, keys_values, keys_values, probs, grad_attn)
+
+
+def stream_orders(bits):
+    if bits == 4:
+        return ((0, 1, 2, 3), (1, 2, 0, 3), (2, 0, 1, 3))
+    return tuple(tuple((t + s) % bits for t in range(bits)) for s in range(3))
+
+
+def sum_kernel(orders, cuts, x_ref, out_ref, acc, twin, held, whole, send_sem, recv_sem):
+    expert, shard = lax.axis_index("expert"), lax.axis_index("shard")
+    units = acc.shape[0]
+    bits = len(orders[0])
+    my_bits = [lax.rem(expert // (1 << b), 2) for b in range(bits)]
+    partners = [expert + (1 << b) * (1 - 2 * my_bits[b]) for b in range(bits)]
+
+    barrier = pltpu.get_barrier_semaphore()
+    pl.semaphore_signal(barrier, inc=1, device_id=(expert, 1 - shard), device_id_type=MESH)
+    for b in range(bits):
+        pl.semaphore_signal(barrier, inc=1, device_id=(partners[b], shard), device_id_type=MESH)
+    pl.semaphore_wait(barrier, bits + 1)
+
+    def copy(source, target, stream, step, device):
+        return pltpu.make_async_remote_copy(
+            src_ref=source,
+            dst_ref=target,
+            send_sem=send_sem.at[stream, step],
+            recv_sem=recv_sem.at[stream, step],
+            device_id=device,
+            device_id_type=MESH,
+        )
+
+    spans, keeps = [], []
+    for order in orders:
+        low_end, size, sends, kept = 0, units, [], []
+        for b in order:
+            size //= 2
+            sends.append(low_end + (1 - my_bits[b]) * size)
+            low_end = low_end + my_bits[b] * size
+            kept.append(low_end)
+        spans.append(sends)
+        keeps.append(kept)
+
+    def halves(stream, step):
+        size = units >> (step + 1)
+        first = units - 2 * size
+        return size, first
+
+    def begin(stream, step):
+        cols = pl.ds(cuts[stream], cuts[stream + 1] - cuts[stream])
+        if step < 0:
+            moved = copy(
+                x_ref.at[1 - shard, :, :, cols],
+                twin.at[:, :, cols],
+                stream,
+                0,
+                (expert, 1 - shard),
+            )
+        elif step < bits:
+            size, first = halves(stream, step)
+            moved = copy(
+                acc.at[pl.ds(spans[stream][step], size), :, cols],
+                held.at[pl.ds(first, size), :, cols],
+                stream,
+                1 + step,
+                (partners[orders[stream][step]], shard),
+            )
+        else:
+            back = 2 * bits - 1 - step
+            size, _ = halves(stream, back)
+            block = whole.at[pl.ds(keeps[stream][back], size), :, cols]
+            moved = copy(block, block, stream, 1 + step, (partners[orders[stream][back]], shard))
+        moved.start()
+        return moved
+
+    def add(stream, step):
+        cols = slice(cuts[stream], cuts[stream + 1])
+        if step < 0:
+
+            def one(unit, carry):
+                total = x_ref[shard, unit, :, cols].astype(jnp.float32) + twin[
+                    unit, :, cols
+                ].astype(jnp.float32)
+                acc[unit, :, cols] = total.astype(acc.dtype)
+                return carry
+
+            lax.fori_loop(0, units, one, 0)
+        elif step < bits:
+            size, first = halves(stream, step)
+            base = keeps[stream][step]
+            target = whole if step == bits - 1 else acc
+
+            def one(unit, carry):
+                total = acc[base + unit, :, cols].astype(jnp.float32) + held[
+                    first + unit, :, cols
+                ].astype(jnp.float32)
+                target[base + unit, :, cols] = total.astype(acc.dtype)
+                return carry
+
+            lax.fori_loop(0, size, one, 0)
+
+    streams = range(len(orders))
+    moving = [begin(s, -1) for s in streams]
+    for step in range(-1, 2 * bits):
+        for s in streams:
+            moving[s].wait()
+            add(s, step)
+            if step + 1 < 2 * bits:
+                moving[s] = begin(s, step + 1)
+
+    def give(unit, carry):
+        out_ref[unit] = whole[unit]
+        return carry
+
+    lax.fori_loop(0, units, give, 0)
+
+
+def sum_over_all(packed, bits):
+    shards, units, rows, columns = packed.shape
+    groups = columns // 128
+    cuts = [0, groups // 3 * 128, 2 * (groups // 3) * 128, columns]
+    orders = stream_orders(bits)
+    steps = 2 * bits + 1
+    return pl.pallas_call(
+        functools.partial(sum_kernel, orders, cuts),
+        out_shape=jax.ShapeDtypeStruct((units, rows, columns), packed.dtype),
+        in_specs=[pl.BlockSpec(memory_space=pltpu.VMEM)],
+        out_specs=pl.BlockSpec(memory_space=pltpu.VMEM),
+        scratch_shapes=[
+            pltpu.VMEM((units, rows, columns), packed.dtype),
+            pltpu.VMEM((units, rows, columns), packed.dtype),
+            pltpu.VMEM((units, rows, columns), packed.dtype),
+            pltpu.VMEM((units, rows, columns), packed.dtype),
+            pltpu.SemaphoreType.DMA((3, steps)),
+            pltpu.SemaphoreType.DMA((3, steps)),
+        ],
+        compiler_params=pltpu.CompilerParams(
+            collective_id=0, has_side_effects=True, vmem_limit_bytes=40 << 20
+        ),
+        name="sum_over_all",
+    )(packed)
 
 
 def on_device(
@@ -323,14 +464,6 @@
     grad_hidden = grad_out + grad_hidden_norm
     grad_branch = grad_hidden.astype(low)
 
-    def whole_sum(parts):
-        packed = jnp.concatenate([part.astype(low) for part in parts], axis=1)
-        extra = -packed.shape[1] % 128
-        packed = jnp.pad(packed, ((0, 0), (0, extra)))
-        halves = lax.psum_scatter(packed, "shard", scatter_dimension=0, tiled=True)
-        return lax.psum(halves, "expert").astype(f32)
-
-    first_sum = whole_sum([dot_tn(attn_part, grad_branch), grad_router, grad_gain_two[:, None]])
     grad_attn = dot_nt(grad_branch, output_weight).astype(low)
     grad_queries, grad_k_part, grad_v_part, folded = attend_backward(
         queries, keys_values, probs, grad_attn, head_size, lanes
@@ -351,20 +484,39 @@
     grad_normed_one = dot_nt(grad_qkv, qkv_weight)
     grad_x_norm, grad_gain_one = rms_backward(x_float, scale_one, gain_one, grad_normed_one)
     grad_tokens = grad_hidden + grad_x_norm
-    second_sum = whole_sum([dot_tn(normed_low, grad_qkv), grad_gain_one[:, None], table_column])
+    narrow = [grad_router, grad_gain_two[:, None], grad_gain_one[:, None], table_column]
+    parts = [dot_tn(normed_low, grad_qkv), dot_tn(attn_part, grad_branch)] + narrow
+    used = sum(part.shape[1] for part in parts)
+    parts.append(jnp.zeros((width, -used % 256), low))
+    packed = jnp.concatenate([part.astype(low) for part in parts], axis=1)
+    total_columns = packed.shape[1]
+    devices = lax.axis_size("expert")
+    bits = devices.bit_length() - 1
+    unit_rows = shard_count * half_width // devices
+    if devices == 1 << bits and unit_rows % 16 == 0:
+        packed = packed.reshape(shard_count, half_width, 2, total_columns // 2)
+        packed = packed.transpose(0, 2, 1, 3).reshape(shard_count, devices, unit_rows, -1)
+        summed = sum_over_all(packed, bits).reshape(2, half_width, -1)
+        summed = jnp.concatenate([summed[0], summed[1]], axis=1)
+    else:
+        halves = lax.psum_scatter(packed, "shard", scatter_dimension=0, tiled=True)
+        summed = lax.psum(halves, "expert")
+    summed = summed.astype(f32)
+    weights_end = 3 * inner + width
+    router_end = weights_end + experts
     grad_w_out = dot_tn(act_low, grad_rows)
     grad_w_in = dot_tn(expert_rows, grad_pre)
     return (
         layer_out,
         grad_tokens,
-        second_sum[:, :inner],
-        second_sum[:, inner : 2 * inner],
-        second_sum[:, 2 * inner : 3 * inner],
-        first_sum[:, :width],
-        first_sum[:, width : width + experts],
-        second_sum[:, 3 * inner],
-        first_sum[:, width + experts],
-        second_sum[: half_buckets * heads, 3 * inner + 1].reshape(half_buckets, heads),
+        summed[:, :inner],
+        summed[:, inner : 2 * inner],
+        summed[:, 2 * inner : 3 * inner],
+        summed[:, 3 * inner : weights_end],
+        summed[:, weights_end:router_end],
+        summed[:, router_end + 1],
+        summed[:, router_end],
+        summed[: half_buckets * heads, router_end + 2].reshape(half_buckets, heads),
         grad_w_in[None],
         grad_w_out[None],
     )

time: 409 us -> 352 us (0.86)
  waiting for transfers between devices: 210 us -> 67.4 us
  Pallas kernels: 21 us -> 84.2 us
  local copies, waits for them, and re-layouts: 39.2 us -> 60 us
    psum x1 -> x0, waiting for transfers between devices: 131 us -> none  [whole_sum(): return lax.psum(halves, 'expert').astype(f32)]
    pallas_call x0 -> x1, Pallas kernels: none -> 63.1 us  [sum_over_all(): pl.pallas_call(functools.partial(sum_kernel, orders, cuts), out_shape=jax...]
    reshape x0 -> x2, local copies, waits for them, and re-layouts: none -> 13.9 us  [on_device(): packed = packed.reshape(shard_count, half_width, 2, total_columns // 2)]
    reduce_scatter x1 -> x0, waiting for transfers between devices: 10.6 us -> none  [whole_sum(): halves = lax.psum_scatter(packed, 'shard', scatter_dimension=0, tiled=True)]
    pad x2 -> x0, local copies, waits for them, and re-layouts: 5.38 us -> none  [whole_sum(): packed = jnp.pad(packed, ((0, 0), (0, extra)))]
    squeeze x0 -> x2, local copies, waits for them, and re-layouts: none -> 4.29 us  [on_device(): summed = jnp.concatenate([summed[0], summed[1]], axis=1)]
    unnamed x122 -> x117, local copies, waits for them, and re-layouts: 15.8 us -> 19.6 us
  transfers between devices with their start and end apart: 14 -> 11, of which waited for: 9 -> 6; matrix products, arithmetic and copies ran while one was open for 19% -> 16% of each run, Pallas kernels for 3% -> 3%
where the time goes in v2:
time: 352 us; the launch traced here: 350 us
  Pallas kernels  84.2 us (24%)
  waiting for transfers between devices  67.4 us (19%)
  matrix products  64.2 us (18%)
  local copies, waits for them, and re-layouts  60 us (17%)
  blocking collectives  27.3 us (8%)
  starting transfers between devices  16.2 us (5%)
  other arithmetic  16.1 us (5%)
  between operations  15 us (4%)
    pallas_call x1, Pallas kernels, sum_over_all(): pl.pallas_call(functools.partial(sum_kernel, orders, cuts), out_shape=jax...  63.1 us
    all_to_all x2, waiting for transfers between devices, collect(): lax.all_to_all(halves, 'expert', split_axis=0, concat_axis=0, tiled=True)  30.7 us
    all_to_all x1, blocking collectives, dispatch(): lax.all_to_all(sent, 'expert', split_axis=0, concat_axis=0, tiled=True)  25.3 us
    dot_general x8, matrix products, dot(): return jnp.dot(a, b, preferred_element_type=f32)  23.2 us
    unnamed x117, local copies, waits for them, and re-layouts  19.6 us
    dot_general x6, matrix products, dot_tn(): return lax.dot_general(a, b, contract_first, preferred_element_type=f32)  19.4 us
    all_to_all x1, waiting for transfers between devices, dispatch(): lax.all_to_all(sent, 'expert', split_axis=0, concat_axis=0, tiled=True)  16 us
    dot_general x4, matrix products, dot_nt(): return lax.dot_general(a, b, contract_last, preferred_element_type=f32)  16 us
  transfers between devices with their start and end apart: 11, of which 6 were waited for; matrix products, arithmetic and copies ran while one was open for 16% of the time, Pallas kernels for 3%

profile of v2, /device:TPU:0, one launch (start us, length us, event | category | flops | bytes accessed | tf_op | source)
XLA Modules:
  0.0 350.5 jit_solution(637699543478205402)
XLA Ops:
  7.3 2.9 pad_maximum_fusion
  10.5 1.9 all_gather.18
  13.2 12.6 %all-gather.6.cloned.1.call-done = bf16[768,2304]{1,0:T(8,128)(2,1)} async-done(((bf16[384,2304]{1,0:T(8,128)(2,1)}), bf16[768,2304]{1,0:T(8,128)(2,1)}) %all-gather.6.cloned.1.call-update) | async-done | bytes 3538960 | tf_op jit(solution)/shard_map/all_gather | solution.py:374
  25.8 3.4 convolution_convert_fusion.1
  33.8 1.8 convolution_convert_fusion.6.q_ref
  35.6 4.7 %all-gather.8.cloned.1.call-done.k_ref.v_ref = bf16[512,1536]{1,0:T(8,128)(2,1)} async-done(((bf16[256,1536]{1,0:T(8,128)(2,1)}), bf16[512,1536]{1,0:T(8,128)(2,1)}) %all-gather.8.cloned.1.call-update) | async-done | bytes 1572880 | tf_op jit(solution)/shard_map/all_gather | solution.py:391
  40.3 1.4 copy-done.2
  42.6 11.6 %attend_forward.1 = (bf16[256,768]{1,0:T(8,128)(2,1)S(1)}, f32[12,256,512]{2,1,0:T(8,128)S(1)}) custom-call(bf16[256,768]{1,0:T(8,128)(2,1)S(1)} %convolution_convert_fusion.6.q_ref, bf16[512,1536]{1,0:T(8,128)(2,1)S(1)} %copy-done.2, bf16[512,1536]{1,0:T(8,128)(2,1)S(1)} %copy-done.2, f32[12,8,768]{2,1,0:T(8,128)S(1)} %stack.35.seed_ref, ...), custom_call_target="tpu_custom_call" | custom-call | flops 402653184 | bytes 8388608 | tf_op jit(solution)/shard_map/attend_forward/pallas_call | solution.py:125
  54.3 2.6 copy-done.4
  56.9 2.7 multiply_reduce_fusion.2
  60.2 2.6 convolution_convert_fusion.4
  62.8 6.8 %all-to-all-start = ((bf16[16,32,768]{2,1,0:T(8,128)(2,1)}), bf16[16,32,768]{2,1,0:T(8,128)(2,1)}, u32[]{:S(2)}, u32[]{:S(2)}) async-start(bf16[16,32,768]{2,1,0:T(8,128)(2,1)} %bitcast.120), calls=%async_computation | async-start | bytes 1572864 | tf_op jit(solution)/shard_map/all_to_all | solution.py:430
  69.7 1.8 fusion.120
  73.8 16.0 %all-to-all-done = bf16[16,32,768]{2,1,0:T(8,128)(2,1)} async-done(((bf16[16,32,768]{2,1,0:T(8,128)(2,1)}), bf16[16,32,768]{2,1,0:T(8,128)(2,1)}, u32[]{:S(2)}, u32[]{:S(2)}) %all-to-all-start) | async-done | bytes 786464 | tf_op jit(solution)/shard_map/all_to_all | solution.py:430
  91.2 25.3 %all_to_all.20 = bf16[16,32,768]{2,1,0:T(8,128)(2,1)} all-to-all(bf16[16,32,768]{2,1,0:T(8,128)(2,1)S(1)} %bitcast.121), channel_id=1, replica_groups=mesh['expert'=16,'shard'=2] {'expert'}, dimensions={0} | all-to-all | bytes 1572864 | tf_op jit(solution)/shard_map/all_to_all | solution.py:430
  116.6 6.7 %multiply_convert_fusion = (bf16[1024,1536]{1,0:T(8,128)(2,1)S(1)}, f32[1024,1536]{1,0:T(8,128)}) fusion(bf16[1024,768]{1,0:T(8,128)(2,1)} %bitcast.123, bf16[1,768,1536]{2,1,0:T(8,128)(2,1)S(1)} %copy-done), kind=kOutput, calls=%fused_computation.9 | convolution fusion | flops 2430074880 | bytes 13369344 | tf_op jit(solution)/shard_map/dot_general | solution.py:360
  123.4 1.7 copy-done.51
  125.0 3.7 %fusion.18 = bf16[32,32,768]{2,1,0:T(8,128)(2,1)} fusion(bf16[32,32,1536]{2,1,0:T(8,128)(2,1)S(1)} %bitcast.142, bf16[1,1536,768]{2,1,0:T(8,128)(2,1)S(1)} %copy-done.48), kind=kOutput, calls=%fused_computation.31 | convolution fusion | flops 2416705536 | bytes 7077888 | tf_op jit(solution)/shard_map/dot_general | solution.py:360
  129.0 8.4 %fusion.6 = bf16[1024,1536]{1,0:T(8,128)(2,1)S(1)} fusion(f32[1024,1536]{1,0:T(8,128)} %get-tuple-element.113, bf16[1024,768]{1,0:T(8,128)(2,1)} %bitcast.139, bf16[1,1536,768]{2,1,0:T(8,128)(2,1)} %param.27), kind=kOutput, calls=%fused_computation.8 | convolution fusion | flops 2447376384 | bytes 13369344 | tf_op jit(solution)/shard_map/dot_general | solution.py:366
  137.4 1.7 copy-done.16
  139.0 3.8 %fusion.21 = bf16[32,32,768]{2,1,0:T(8,128)(2,1)} fusion(bf16[32,32,1536]{2,1,0:T(8,128)(2,1)S(1)} %bitcast.122, bf16[1,768,1536]{2,1,0:T(8,128)(2,1)S(1)} %copy-done), kind=kOutput, calls=%fused_computation.32 | convolution fusion | flops 2416705536 | bytes 7077888 | tf_op jit(solution)/shard_map/dot_general | solution.py:366
  142.9 4.3 %all-to-all-start.1 = ((bf16[16,32,768]{2,1,0:T(8,128)(2,1)}), bf16[16,32,768]{2,1,0:T(8,128)(2,1)}, u32[]{:S(2)}, u32[]{:S(2)}) async-start(bf16[16,32,768]{2,1,0:T(8,128)(2,1)} %reduce-scatter.4.cloned.1.call-done), calls=%async_computation.2 | async-start | bytes 1572864 | tf_op jit(solution)/shard_map/all_to_all | solution.py:440
  147.2 2.5 reduce-scatter.6.cloned.1.call-done
  149.8 16.0 %all-to-all-done.1 = bf16[16,32,768]{2,1,0:T(8,128)(2,1)} async-done(((bf16[16,32,768]{2,1,0:T(8,128)(2,1)}), bf16[16,32,768]{2,1,0:T(8,128)(2,1)}, u32[]{:S(2)}, u32[]{:S(2)}) %all-to-all-start.1) | async-done | bytes 786464 | tf_op jit(solution)/shard_map/all_to_all | solution.py:440
  165.8 4.6 %all-to-all-start.3 = ((bf16[16,32,768]{2,1,0:T(8,128)(2,1)}), bf16[16,32,768]{2,1,0:T(8,128)(2,1)}, u32[]{:S(2)}, u32[]{:S(2)}) async-start(bf16[16,32,768]{2,1,0:T(8,128)(2,1)} %reduce-scatter.6.cloned.1.call-done), calls=%async_computation.5 | async-start | bytes 1572864 | tf_op jit(solution)/shard_map/all_to_all | solution.py:440
  170.4 2.4 fusion.26
  172.9 1.4 fusion.87
  174.3 14.7 %all-to-all-done.3 = bf16[16,32,768]{2,1,0:T(8,128)(2,1)} async-done(((bf16[16,32,768]{2,1,0:T(8,128)(2,1)}), bf16[16,32,768]{2,1,0:T(8,128)(2,1)}, u32[]{:S(2)}, u32[]{:S(2)}) %all-to-all-start.3) | async-done | bytes 786464 | tf_op jit(solution)/shard_map/all_to_all | solution.py:440
  189.0 2.3 multiply_reduce_fusion
  191.4 2.3 convert_add_fusion.1
  194.3 9.6 %attend_backward.1 = (bf16[256,768]{1,0:T(8,128)(2,1)S(1)}, bf16[512,768]{1,0:T(8,128)(2,1)S(1)}, bf16[512,768]{1,0:T(8,128)(2,1)S(1)}, f32[12,8,768]{2,1,0:T(8,128)S(1)}) custom-call(bf16[256,768]{1,0:T(8,128)(2,1)S(1)} %convolution_convert_fusion.6.q_ref, bf16[512,1536]{1,0:T(8,128)(2,1)S(1)} %copy-done.3, bf16[512,1536]{1,0:T(8,128)(2,1)S(1)} %copy-done.3, ...), custom_call_target="tpu_custom_call" | custom-call | flops 805306368 | bytes 9437184 | tf_op jit(solution)/shard_map/attend_backward/pallas_call | solution.py:160
  206.6 6.9 %convolution_bitcast_fusion = f32[1,1536,768]{2,1,0:T(8,128)} fusion(bf16[1024,1536]{1,0:T(8,128)(2,1)} %copy-done.51, bf16[1024,768]{1,0:T(8,128)(2,1)S(1)} %bitcast.140), kind=kOutput, calls=%fused_computation.11 | convolution fusion | flops 2415919104 | bytes 9437184 | tf_op jit(solution)/shard_map/dot_general | solution.py:363
  213.5 4.4 %convolution_bitcast_fusion.1 = f32[1,768,1536]{2,1,0:T(8,128)} fusion(bf16[1024,768]{1,0:T(8,128)(2,1)S(1)} %bitcast.124, bf16[1024,1536]{1,0:T(8,128)(2,1)S(1)} %copy-done.17), kind=kOutput, calls=%fused_computation.12 | convolution fusion | flops 2415919104 | bytes 9437184 | tf_op jit(solution)/shard_map/dot_general | solution.py:363
  220.1 1.8 convolution_convert_fusion.7
  224.3 1.5 convolution_convert_fusion.2
  225.8 2.1 constant_dynamic-update-slice_fusion
  227.9 2.8 convolution_convert_fusion
  230.7 3.3 fusion.36
  235.6 8.0 %concatenate.92 = bf16[768,3328]{1,0:T(8,128)(2,1)} concatenate(bf16[768,2304]{1,0:T(8,128)(2,1)S(1)} %convolution_convert_fusion, bf16[768,768]{1,0:T(8,128)(2,1)} %convolution_convert_fusion.2, bf16[768,16]{1,0:T(8,128)(2,1)} %copy.115, bf16[768,1]{1,0:T(8,128)(2,1)} %convert_element_type.245, bf16[768,1]{1,0:T(8,128)(2,1)} %convert_element_type.246, bf16[768,1]{1,0:T(8,128)(2,1)} %bitcast.125, ...), dimensions={1} | concatenate | bytes 10223616 | tf_op jit(solution)/shard_map/concatenate | solution.py:491
  243.6 10.8 %reshape.220 = bf16[2,384,2,1664]{3,2,1,0:T(2,128)(2,1)} reshape(bf16[768,3328]{1,0:T(8,128)(2,1)} %concatenate.92) | data formatting | bytes 10223616 | tf_op jit(solution)/shard_map/reshape | solution.py:497
  254.4 3.1 copy.119
  257.5 63.1 %sum_over_all.1 = bf16[16,48,1664]{2,1,0:T(8,128)(2,1)S(1)} custom-call(bf16[2,16,48,1664]{3,2,1,0:T(8,128)(2,1)S(1)} %bitcast.107), custom_call_target="tpu_custom_call" | custom-call | tf_op jit(solution)/shard_map/sum_over_all/pallas_call | solution.py:310
  321.8 1.7 copy.120
  323.5 2.6 copy.121
  327.4 2.6 maximum_convert_fusion
  330.7 3.7 %fusion.118 = (f32[384,768]{0,1:T(8,128)}, f32[384,768]{0,1:T(8,128)S(1)}, f32[384,768]{0,1:T(8,128)S(1)}, f32[384,768]{0,1:T(8,128)S(1)}) fusion(f32[384,3328]{0,1:T(8,128)} %maximum_convert_fusion), kind=kLoop, calls=%fused_computation.184 | loop fusion | bytes 9437184 | tf_op jit(solution)/shard_map/slice | solution.py:515
  338.5 2.8 copy.125
  341.4 2.3 fusion.33
  (217 shorter events, 27.9 us)
Async XLA Ops:
  7.2 109.4 %copy-start = (bf16[1,768,1536]{2,1,0:T(8,128)(2,1)S(1)}, bf16[1,768,1536]{2,1,0:T(8,128)(2,1)}, u32[]{:S(2)}) copy-start(bf16[1,768,1536]{2,1,0:T(8,128)(2,1)} %param.26) | copy-start | bytes 7077892
  7.2 3.1 copy-start.43
  7.2 3.2 copy-start.45
  7.2 3.2 copy-start.46
  7.2 3.2 copy-start.41
  7.2 5.2 %copy-start.11 = (bf16[256,768]{1,0:T(8,128)(2,1)S(1)}, bf16[256,768]{1,0:T(8,128)(2,1)}, u32[]{:S(2)}) copy-start(bf16[256,768]{1,0:T(8,128)(2,1)} %param.14) | copy-start | bytes 1179652
  7.2 18.5 %all-gather.6.cloned.1.call-start = ((), (), s32[]{:S(2)}) async-start(), calls=%async_computation.7 | async-start | bytes 5308416 | tf_op jit(solution)/shard_map/all_gather | solution.py:374
  10.2 30.1 %all-gather.8.cloned.1.call-start = ((), (), s32[]{:S(2)}) async-start(), calls=%async_computation.8 | async-start | bytes 2359296 | tf_op jit(solution)/shard_map/all_gather | solution.py:391
  12.4 17.5 %copy-start.20 = (bf16[768,19]{0,1:T(8,128)(2,1)}, bf16[768,19]{0,1:T(8,128)(2,1)S(1)}, u32[]{:S(2)}) copy-start(bf16[768,19]{0,1:T(8,128)(2,1)S(1)} %all_gather.18) | copy-start | bytes 87556
  12.5 21.3 %copy-start.22 = (f32[768]{0:T(1024)}, f32[768]{0:T(1024)S(1)}, u32[]{:S(2)}) copy-start(f32[768]{0:T(1024)S(1)} %get-tuple-element.91) | copy-start | bytes 9220
  12.5 47.7 %copy-start.24 = (f32[768]{0:T(1024)}, f32[768]{0:T(1024)S(1)}, u32[]{:S(2)}) copy-start(f32[768]{0:T(1024)S(1)} %get-tuple-element.90) | copy-start | bytes 9220
  13.2 20.6 %copy-start.33 = (f32[256]{0:T(256)}, f32[256]{0:T(256)S(1)}, u32[]{:S(2)}) copy-start(f32[256]{0:T(256)S(1)} %get-tuple-element.107) | copy-start | bytes 3076
  29.2 4.4 %copy-start.35 = (s32[256,1]{0,1:T(1,128)S(1)}, s32[256,1]{0,1:T(1,128)}, u32[]{:S(2)}) copy-start(s32[256,1]{0,1:T(1,128)} %param.17) | copy-start | bytes 3076
  29.2 27.7 %all-gather.10.cloned.1.call-start = ((), (), s32[]{:S(2)}) async-start(), calls=%async_computation.9 | async-start | bytes 1769472 | tf_op jit(solution)/shard_map/all_gather | solution.py:377
  33.8 26.4 %copy-start.28 = (s32[256,1]{0,1:T(1,128)}, s32[256,1]{0,1:T(1,128)S(1)}, u32[]{:S(2)}) copy-start(s32[256,1]{0,1:T(1,128)S(1)} %multiply_add_fusion) | copy-start | bytes 3076
  59.6 30.2 %copy-start.15 = (bf16[256,768]{1,0:T(8,128)(2,1)S(1)}, bf16[256,768]{1,0:T(8,128)(2,1)}, u32[]{:S(2)}) copy-start(bf16[256,768]{1,0:T(8,128)(2,1)} %param.15) | copy-start | bytes 1179652
  62.8 27.0 %all-to-all-start = ((bf16[16,32,768]{2,1,0:T(8,128)(2,1)}), bf16[16,32,768]{2,1,0:T(8,128)(2,1)}, u32[]{:S(2)}, u32[]{:S(2)}) async-start(bf16[16,32,768]{2,1,0:T(8,128)(2,1)} %bitcast.120), calls=%async_computation | async-start | bytes 1572864 | tf_op jit(solution)/shard_map/all_to_all | solution.py:430
  69.6 46.9 %all-gather.12.cloned.1.call-start = ((), (), s32[]{:S(2)}) async-start(), calls=%async_computation.10 | async-start | bytes 2359296 | tf_op jit(solution)/shard_map/all_gather | solution.py:431
  89.8 39.1 %all-gather.14.cloned.1.call-start = ((), (), s32[]{:S(2)}) async-start(), calls=%async_computation.12 | async-start | bytes 2359296 | tf_op jit(solution)/shard_map/all_gather | solution.py:431
  116.5 26.4 %reduce-scatter.4.cloned.1.call-start = ((), (), s32[]{:S(2)}) async-start(), calls=%async_computation.11 | async-start | bytes 2359296 | tf_op jit(solution)/shard_map/reduce_scatter | solution.py:434
  116.6 8.4 %copy-start.48 = (bf16[1,1536,768]{2,1,0:T(8,128)(2,1)S(1)}, bf16[1,1536,768]{2,1,0:T(8,128)(2,1)}, u32[]{:S(2)}) copy-start(bf16[1,1536,768]{2,1,0:T(8,128)(2,1)} %param.27) | copy-start | bytes 7077892
  128.7 21.1 %reduce-scatter.6.cloned.1.call-start = ((), (), s32[]{:S(2)}) async-start(), calls=%async_computation.13 | async-start | bytes 2359296 | tf_op jit(solution)/shard_map/reduce_scatter | solution.py:434
  142.8 27.6 %copy-start.29 = (s32[256,1]{0,1:T(1,128)S(1)}, s32[256,1]{0,1:T(1,128)}, u32[]{:S(2)}) copy-start(s32[256,1]{0,1:T(1,128)} %copy-done.28) | copy-start | bytes 3076
  142.8 30.1 %copy-start.21 = (bf16[768,19]{0,1:T(8,128)(2,1)S(1)}, bf16[768,19]{0,1:T(8,128)(2,1)}, u32[]{:S(2)}) copy-start(bf16[768,19]{0,1:T(8,128)(2,1)} %copy-done.20) | copy-start | bytes 87556
  142.8 30.0 %copy-start.31 = (f32[256]{0:T(256)S(1)}, f32[256]{0:T(256)}, u32[]{:S(2)}) copy-start(f32[256]{0:T(256)} %copy-done.30) | copy-start | bytes 3076
  142.8 30.0 %copy-start.32 = (f32[256]{0:T(256)S(1)}, f32[256]{0:T(256)}, u32[]{:S(2)}) copy-start(f32[256]{0:T(256)} %multiply_reduce_fusion.3) | copy-start | bytes 3076
  142.9 30.0 %copy-start.36 = (s32[256,1]{0,1:T(1,128)S(1)}, s32[256,1]{0,1:T(1,128)}, u32[]{:S(2)}) copy-start(s32[256,1]{0,1:T(1,128)} %param.17) | copy-start | bytes 3076
  142.9 30.0 %copy-start.38 = (f32[256]{0:T(256)S(1)}, f32[256]{0:T(256)}, u32[]{:S(2)}) copy-start(f32[256]{0:T(256)} %copy-done.37) | copy-start | bytes 3076
  142.9 22.8 %all-to-all-start.1 = ((bf16[16,32,768]{2,1,0:T(8,128)(2,1)}), bf16[16,32,768]{2,1,0:T(8,128)(2,1)}, u32[]{:S(2)}, u32[]{:S(2)}) async-start(bf16[16,32,768]{2,1,0:T(8,128)(2,1)} %reduce-scatter.4.cloned.1.call-done), calls=%async_computation.2 | async-start | bytes 1572864 | tf_op jit(solution)/shard_map/all_to_all | solution.py:440
  147.2 41.8 %copy-start.25 = (f32[768]{0:T(1024)S(1)}, f32[768]{0:T(1024)}, u32[]{:S(2)}) copy-start(f32[768]{0:T(1024)} %copy-done.24) | copy-start | bytes 9220
  147.2 41.8 %copy-start.27 = (f32[256]{0:T(256)S(1)}, f32[256]{0:T(256)}, u32[]{:S(2)}) copy-start(f32[256]{0:T(256)} %copy-done.26) | copy-start | bytes 3076
  165.7 28.5 %slice-start = ((s8[6291456]{0:T(1024)(128)(4,1)}), s8[2097152]{0:T(1024)(128)(4,1)S(1)}, s32[]{:S(2)}) async-start(s8[6291456]{0:T(1024)(128)(4,1)} %bitcast.108), calls=%async_computation.15 | async-start | bytes 4194304
  165.8 23.2 %all-to-all-start.3 = ((bf16[16,32,768]{2,1,0:T(8,128)(2,1)}), bf16[16,32,768]{2,1,0:T(8,128)(2,1)}, u32[]{:S(2)}, u32[]{:S(2)}) async-start(bf16[16,32,768]{2,1,0:T(8,128)(2,1)} %reduce-scatter.6.cloned.1.call-done), calls=%async_computation.5 | async-start | bytes 1572864 | tf_op jit(solution)/shard_map/all_to_all | solution.py:440
  170.4 55.4 %reduce-scatter.8.cloned.1.call-start = ((), (), s32[]{:S(2)}) async-start(), calls=%async_computation.14 | async-start | bytes 2359296 | tf_op jit(solution)/shard_map/reduce_scatter | solution.py:471
  170.4 20.9 %copy-start.44 = (f32[256]{0:T(256)S(1)}, f32[256]{0:T(256)}, u32[]{:S(2)}) copy-start(f32[256]{0:T(256)} %get-tuple-element.108) | copy-start | bytes 3076
  189.0 5.2 %slice-start.1 = ((s8[6291456]{0:T(1024)(128)(4,1)}), s8[4194304]{0:T(1024)(128)(4,1)S(1)}, s32[]{:S(2)}) async-start(s8[6291456]{0:T(1024)(128)(4,1)} %bitcast.108), calls=%async_computation.16 | async-start | bytes 8388608
  193.7 10.1 %copy-start.8 = (f32[256,768]{1,0:T(8,128)}, f32[256,768]{1,0:T(8,128)S(1)}, u32[]{:S(2)}) copy-start(f32[256,768]{1,0:T(8,128)S(1)} %get-tuple-element.98) | copy-start | bytes 2359300
  206.5 6.9 %copy-start.17 = (bf16[1024,1536]{1,0:T(8,128)(2,1)S(1)}, bf16[1024,1536]{1,0:T(8,128)(2,1)}, u32[]{:S(2)}) copy-start(bf16[1024,1536]{1,0:T(8,128)(2,1)} %copy-done.16) | copy-start | bytes 9437188
  206.5 6.9 %copy-start.19 = (bf16[32,32,768]{2,1,0:T(8,128)(2,1)S(1)}, bf16[32,32,768]{2,1,0:T(8,128)(2,1)}, u32[]{:S(2)}) copy-start(bf16[32,32,768]{2,1,0:T(8,128)(2,1)} %all-gather.12.cloned.1.call-done) | copy-start | bytes 4718596
  213.4 4.4 %copy-start.7 = (f32[12,8,768]{2,1,0:T(8,128)S(1)}, f32[12,8,768]{2,1,0:T(8,128)}, u32[]{:S(2)}) copy-start(f32[12,8,768]{2,1,0:T(8,128)} %copy-done.6) | copy-start | bytes 884740
  213.5 5.1 %copy-start.40 = (s32[768]{0:T(1024)S(1)}, s32[768]{0:T(1024)}, u32[]{:S(2)}) copy-start(s32[768]{0:T(1024)} %copy-done.39) | copy-start | bytes 9220
  217.8 6.5 %copy-start.9 = (f32[256,768]{1,0:T(8,128)S(1)}, f32[256,768]{1,0:T(8,128)}, u32[]{:S(2)}) copy-start(f32[256,768]{1,0:T(8,128)} %copy-done.8) | copy-start | bytes 2359300
  221.8 6.1 %copy-start.23 = (f32[768]{0:T(1024)S(1)}, f32[768]{0:T(1024)}, u32[]{:S(2)}) copy-start(f32[768]{0:T(1024)} %copy-done.22) | copy-start | bytes 9220
  221.8 6.1 %copy-start.34 = (f32[256]{0:T(256)S(1)}, f32[256]{0:T(256)}, u32[]{:S(2)}) copy-start(f32[256]{0:T(256)} %copy-done.33) | copy-start | bytes 3076
  337.2 4.2 %copy-start.10 = (f32[256,768]{1,0:T(8,128)S(1)}, f32[256,768]{1,0:T(8,128)}, u32[]{:S(2)}) copy-start(f32[256,768]{1,0:T(8,128)} %copy-done.8) | copy-start | bytes 2359300
  337.2 4.2 %copy-start.13 = (bf16[256,768]{1,0:T(8,128)(2,1)S(1)}, bf16[256,768]{1,0:T(8,128)(2,1)}, u32[]{:S(2)}) copy-start(bf16[256,768]{1,0:T(8,128)(2,1)} %param.14) | copy-start | bytes 1179652
  337.2 4.2 %copy-start.42 = (f32[256]{0:T(256)S(1)}, f32[256]{0:T(256)}, u32[]{:S(2)}) copy-start(f32[256]{0:T(256)} %get-tuple-element.106) | copy-start | bytes 3076
  338.5 5.1 %copy-start.1 = (bf16[1,768,1536]{2,1,0:T(8,128)(2,1)S(1)}, bf16[1,768,1536]{2,1,0:T(8,128)(2,1)}, u32[]{:S(2)}) copy-start(bf16[1,768,1536]{2,1,0:T(8,128)(2,1)} %param.26) | copy-start | bytes 7077892
  (17 other events, 31.1 us)
Sparse Core Ops, SparseCore 0:
  10.3 15.3 all-gather.5
  29.3 10.9 all-gather.7
  41.9 10.4 all-gather.9
  89.9 9.2 all-gather.11
  116.6 7.5 all-gather.13
  128.8 8.2 reduce-scatter.3
  142.9 6.7 reduce-scatter.5
  206.0 8.3 reduce-scatter.7

commit v3 on v2

--- a/solution.py
+++ b/solution.py
@@ -193,7 +193,7 @@
     return tuple(tuple((t + s) % bits for t in range(bits)) for s in range(3))
 
 
-def sum_kernel(orders, cuts, x_ref, out_ref, acc, twin, held, whole, send_sem, recv_sem):
+def sum_kernel(orders, cuts, first_ref, second_ref, first_out, second_out, acc, twin, held, whole, send_sem, recv_sem):
     expert, shard = lax.axis_index("expert"), lax.axis_index("shard")
     units = acc.shape[0]
     bits = len(orders[0])
@@ -235,13 +235,15 @@
     def begin(stream, step):
         cols = pl.ds(cuts[stream], cuts[stream + 1] - cuts[stream])
         if step < 0:
-            moved = copy(
-                x_ref.at[1 - shard, :, :, cols],
-                twin.at[:, :, cols],
-                stream,
-                0,
-                (expert, 1 - shard),
+            mate = (expert, 1 - shard)
+            lower, upper = twin.at[: units // 2], twin.at[units // 2 :]
+            extra = copy(
+                first_ref.at[1 - shard, :, :, cols], lower.at[:, :, cols], stream, 2 * bits + 1, mate
             )
+            extra.start()
+            moved = copy(second_ref.at[1 - shard, :, :, cols], upper.at[:, :, cols], stream, 0, mate)
+            moved.start()
+            return (extra, moved)
         elif step < bits:
             size, first = halves(stream, step)
             moved = copy(
@@ -257,20 +259,22 @@
             block = whole.at[pl.ds(keeps[stream][back], size), :, cols]
             moved = copy(block, block, stream, 1 + step, (partners[orders[stream][back]], shard))
         moved.start()
-        return moved
+        return (moved,)
 
     def add(stream, step):
         cols = slice(cuts[stream], cuts[stream + 1])
         if step < 0:
 
-            def one(unit, carry):
-                total = x_ref[shard, unit, :, cols].astype(jnp.float32) + twin[
-                    unit, :, cols
-                ].astype(jnp.float32)
-                acc[unit, :, cols] = total.astype(acc.dtype)
-                return carry
-
-            lax.fori_loop(0, units, one, 0)
+            for number, ref in enumerate((first_ref, second_ref)):
+
+                def one(unit, carry, ref=ref, base=number * units // 2):
+                    total = ref[shard, unit, :, cols].astype(jnp.float32) + twin[
+                        base + unit, :, cols
+                    ].astype(jnp.float32)
+                    acc[base + unit, :, cols] = total.astype(acc.dtype)
+                    return carry
+
+                lax.fori_loop(0, units // 2, one, 0)
         elif step < bits:
             size, first = halves(stream, step)
             base = keeps[stream][step]
@@ -289,34 +293,37 @@
     moving = [begin(s, -1) for s in streams]
     for step in range(-1, 2 * bits):
         for s in streams:
-            moving[s].wait()
+            for moved in moving[s]:
+                moved.wait()
             add(s, step)
             if step + 1 < 2 * bits:
                 moving[s] = begin(s, step + 1)
 
     def give(unit, carry):
-        out_ref[unit] = whole[unit]
+        first_out[unit] = whole[unit].astype(first_out.dtype)
+        second_out[unit] = whole[units // 2 + unit].astype(second_out.dtype)
         return carry
 
-    lax.fori_loop(0, units, give, 0)
-
-
-def sum_over_all(packed, bits):
-    shards, units, rows, columns = packed.shape
+    lax.fori_loop(0, units // 2, give, 0)
+
+
+def sum_over_all(first, second, bits):
+    shards, blocks, rows, columns = first.shape
+    units = 2 * blocks
     groups = columns // 128
     cuts = [0, groups // 3 * 128, 2 * (groups // 3) * 128, columns]
     orders = stream_orders(bits)
-    steps = 2 * bits + 1
+    steps = 2 * bits + 2
     return pl.pallas_call(
         functools.partial(sum_kernel, orders, cuts),
-        out_shape=jax.ShapeDtypeStruct((units, rows, columns), packed.dtype),
-        in_specs=[pl.BlockSpec(memory_space=pltpu.VMEM)],
-        out_specs=pl.BlockSpec(memory_space=pltpu.VMEM),
+        out_shape=[jax.ShapeDtypeStruct((blocks, rows, columns), jnp.float32)] * 2,
+        in_specs=[pl.BlockSpec(memory_space=pltpu.VMEM)] * 2,
+        out_specs=[pl.BlockSpec(memory_space=pltpu.VMEM)] * 2,
         scratch_shapes=[
-            pltpu.VMEM((units, rows, columns), packed.dtype),
-            pltpu.VMEM((units, rows, columns), packed.dtype),
-            pltpu.VMEM((units, rows, columns), packed.dtype),
-            pltpu.VMEM((units, rows, columns), packed.dtype),
+            pltpu.VMEM((units, rows, columns), first.dtype),
+            pltpu.VMEM((units, rows, columns), first.dtype),
+            pltpu.VMEM((units, rows, columns), first.dtype),
+            pltpu.VMEM((units, rows, columns), first.dtype),
             pltpu.SemaphoreType.DMA((3, steps)),
             pltpu.SemaphoreType.DMA((3, steps)),
         ],
@@ -324,7 +331,7 @@
             collective_id=0, has_side_effects=True, vmem_limit_bytes=40 << 20
         ),
         name="sum_over_all",
-    )(packed)
+    )(first, second)
 
 
 def on_device(
@@ -485,38 +492,44 @@
     grad_x_norm, grad_gain_one = rms_backward(x_float, scale_one, gain_one, grad_normed_one)
     grad_tokens = grad_hidden + grad_x_norm
     narrow = [grad_router, grad_gain_two[:, None], grad_gain_one[:, None], table_column]
-    parts = [dot_tn(normed_low, grad_qkv), dot_tn(attn_part, grad_branch)] + narrow
-    used = sum(part.shape[1] for part in parts)
-    parts.append(jnp.zeros((width, -used % 256), low))
-    packed = jnp.concatenate([part.astype(low) for part in parts], axis=1)
-    total_columns = packed.shape[1]
+    used = 3 * inner + width + sum(part.shape[1] for part in narrow)
+    half_columns = (used + -used % 256) // 2
+    narrow.append(jnp.zeros((width, -used % 256), low))
+    first = dot_tn(normed_low, grad_qkv[:, :half_columns]).astype(low)
+    second = [dot_tn(normed_low, grad_qkv[:, half_columns:]), dot_tn(attn_part, grad_branch)]
+    second = jnp.concatenate([part.astype(low) for part in second + narrow], axis=1)
     devices = lax.axis_size("expert")
     bits = devices.bit_length() - 1
     unit_rows = shard_count * half_width // devices
     if devices == 1 << bits and unit_rows % 16 == 0:
-        packed = packed.reshape(shard_count, half_width, 2, total_columns // 2)
-        packed = packed.transpose(0, 2, 1, 3).reshape(shard_count, devices, unit_rows, -1)
-        summed = sum_over_all(packed, bits).reshape(2, half_width, -1)
-        summed = jnp.concatenate([summed[0], summed[1]], axis=1)
+        blocks = (shard_count, devices // 2, 2 * half_width // devices, half_columns)
+        first, second = sum_over_all(first.reshape(blocks), second.reshape(blocks), bits)
+        first = first.reshape(half_width, half_columns)
+        second = second.reshape(half_width, half_columns)
     else:
+        packed = jnp.concatenate([first, second], axis=1)
         halves = lax.psum_scatter(packed, "shard", scatter_dimension=0, tiled=True)
-        summed = lax.psum(halves, "expert")
-    summed = summed.astype(f32)
-    weights_end = 3 * inner + width
+        summed = lax.psum(halves, "expert").astype(f32)
+        first, second = summed[:, :half_columns], summed[:, half_columns:]
+    grad_value = jnp.concatenate(
+        [first[:, 2 * inner :], second[:, : 3 * inner - half_columns]], axis=1
+    )
+    second = second[:, 3 * inner - half_columns :]
+    weights_end = width
     router_end = weights_end + experts
     grad_w_out = dot_tn(act_low, grad_rows)
     grad_w_in = dot_tn(expert_rows, grad_pre)
     return (
         layer_out,
         grad_tokens,
-        summed[:, :inner],
-        summed[:, inner : 2 * inner],
-        summed[:, 2 * inner : 3 * inner],
-        summed[:, 3 * inner : weights_end],
-        summed[:, weights_end:router_end],
-        summed[:, router_end + 1],
-        summed[:, router_end],
-        summed[: half_buckets * heads, router_end + 2].reshape(half_buckets, heads),
+        first[:, :inner],
+        first[:, inner : 2 * inner],
+        grad_value,
+        second[:, :weights_end],
+        second[:, weights_end:router_end],
+        second[:, router_end + 1],
+        second[:, router_end],
+        second[: half_buckets * heads, router_end + 2].reshape(half_buckets, heads),
         grad_w_in[None],
         grad_w_out[None],
     )

time: 352 us -> 326 us (0.926)
  local copies, waits for them, and re-layouts: 60 us -> 33.1 us
    reshape x2 -> x0, local copies, waits for them, and re-layouts: 13.9 us -> none  [on_device(): packed = packed.reshape(shard_count, half_width, 2, total_columns // 2)]
    unnamed x117, local copies, waits for them, and re-layouts: 19.6 us -> 14.3 us
    squeeze x2 -> x0, local copies, waits for them, and re-layouts: 4.29 us -> none  [on_device(): summed = jnp.concatenate([summed[0], summed[1]], axis=1)]
    dot_general x6 -> x7, matrix products: 19.4 us -> 21.5 us  [dot_tn(): return lax.dot_general(a, b, contract_first, preferred_element_type=f32)]
  transfers between devices with their start and end apart: 11 -> 11, of which waited for: 6 -> 6; matrix products, arithmetic and copies ran while one was open for 16% -> 17% of each run, Pallas kernels for 3% -> 4%
where the time goes in v3:
time: 326 us; the launch traced here: 325 us
  Pallas kernels  84.3 us (26%)
  waiting for transfers between devices  67.3 us (21%)
  matrix products  66.3 us (20%)
  local copies, waits for them, and re-layouts  33.1 us (10%)
  blocking collectives  27.3 us (8%)
  starting transfers between devices  16.2 us (5%)
  other arithmetic  15 us (5%)
  between operations  15 us (5%)
    pallas_call x1, Pallas kernels, sum_over_all(): pl.pallas_call(functools.partial(sum_kernel, orders, cuts), out_shape=[ja...  63.1 us
    all_to_all x2, waiting for transfers between devices, collect(): lax.all_to_all(halves, 'expert', split_axis=0, concat_axis=0, tiled=True)  30.7 us
    all_to_all x1, blocking collectives, dispatch(): lax.all_to_all(sent, 'expert', split_axis=0, concat_axis=0, tiled=True)  25.3 us
    dot_general x8, matrix products, dot(): return jnp.dot(a, b, preferred_element_type=f32)  23.2 us
    dot_general x7, matrix products, dot_tn(): return lax.dot_general(a, b, contract_first, preferred_element_type=f32)  21.5 us
    dot_general x4, matrix products, dot_nt(): return lax.dot_general(a, b, contract_last, preferred_element_type=f32)  16 us
    all_to_all x1, waiting for transfers between devices, dispatch(): lax.all_to_all(sent, 'expert', split_axis=0, concat_axis=0, tiled=True)  16 us
    unnamed x117, local copies, waits for them, and re-layouts  14.3 us
  transfers between devices with their start and end apart: 11, of which 6 were waited for; matrix products, arithmetic and copies ran while one was open for 17% of the time, Pallas kernels for 4%

profile of v3, /device:TPU:0, one launch (start us, length us, event | category | flops | bytes accessed | tf_op | source)
XLA Modules:
  0.0 324.5 jit_solution(13001132365308543659)
XLA Ops:
  7.3 2.9 pad_maximum_fusion
  10.5 1.9 all_gather.18
  13.2 12.6 %all-gather.6.cloned.1.call-done = bf16[768,2304]{1,0:T(8,128)(2,1)} async-done(((bf16[384,2304]{1,0:T(8,128)(2,1)}), bf16[768,2304]{1,0:T(8,128)(2,1)}) %all-gather.6.cloned.1.call-update) | async-done | bytes 3538960 | tf_op jit(solution)/shard_map/all_gather | solution.py:381
  25.8 3.4 %convolution_convert_fusion.1 = bf16[256,1536]{1,0:T(8,128)(2,1)} fusion(bf16[768,2304]{1,0:T(8,128)(2,1)} %all-gather.6.cloned.1.call-done, bf16[256,768]{1,0:T(8,128)(2,1)S(1)} %copy-done.13, f32[768]{0:T(1024)S(1)} %get-tuple-element.35, f32[256]{0:T(256)S(1)} %get-tuple-element.47), kind=kOutput, calls=%fused_computation.13 | convolution fusion | flops 605159424 | bytes 3543040 | tf_op jit(solution)/shard_map/dot_general | solution.py:367
  33.8 1.8 convolution_convert_fusion.7.q_ref
  35.6 4.7 %all-gather.8.cloned.1.call-done.k_ref.v_ref = bf16[512,1536]{1,0:T(8,128)(2,1)} async-done(((bf16[256,1536]{1,0:T(8,128)(2,1)}), bf16[512,1536]{1,0:T(8,128)(2,1)}) %all-gather.8.cloned.1.call-update) | async-done | bytes 1572880 | tf_op jit(solution)/shard_map/all_gather | solution.py:398
  40.3 1.4 copy-done.2
  42.6 11.6 %attend_forward.1 = (bf16[256,768]{1,0:T(8,128)(2,1)S(1)}, f32[12,256,512]{2,1,0:T(8,128)S(1)}) custom-call(bf16[256,768]{1,0:T(8,128)(2,1)S(1)} %convolution_convert_fusion.7.q_ref, bf16[512,1536]{1,0:T(8,128)(2,1)S(1)} %copy-done.2, bf16[512,1536]{1,0:T(8,128)(2,1)S(1)} %copy-done.2, f32[12,8,768]{2,1,0:T(8,128)S(1)} %stack.35.seed_ref, ...), custom_call_target="tpu_custom_call" | custom-call | flops 402653184 | bytes 8388608 | tf_op jit(solution)/shard_map/attend_forward/pallas_call | solution.py:125
  54.3 2.6 copy-done.5
  56.9 2.7 multiply_reduce_fusion.2
  60.2 2.6 convolution_convert_fusion.5
  62.8 6.8 %all-to-all-start = ((bf16[16,32,768]{2,1,0:T(8,128)(2,1)}), bf16[16,32,768]{2,1,0:T(8,128)(2,1)}, u32[]{:S(2)}, u32[]{:S(2)}) async-start(bf16[16,32,768]{2,1,0:T(8,128)(2,1)} %bitcast.121), calls=%async_computation | async-start | bytes 1572864 | tf_op jit(solution)/shard_map/all_to_all | solution.py:437
  69.7 1.8 fusion.122
  72.6 1.3 multiply_reduce_fusion.3
  73.8 16.0 %all-to-all-done = bf16[16,32,768]{2,1,0:T(8,128)(2,1)} async-done(((bf16[16,32,768]{2,1,0:T(8,128)(2,1)}), bf16[16,32,768]{2,1,0:T(8,128)(2,1)}, u32[]{:S(2)}, u32[]{:S(2)}) %all-to-all-start) | async-done | bytes 786464 | tf_op jit(solution)/shard_map/all_to_all | solution.py:437
  89.9 1.3 convolution_convert_fusion.4
  91.2 25.3 %all_to_all.20 = bf16[16,32,768]{2,1,0:T(8,128)(2,1)} all-to-all(bf16[16,32,768]{2,1,0:T(8,128)(2,1)S(1)} %bitcast.122), channel_id=1, replica_groups=mesh['expert'=16,'shard'=2] {'expert'}, dimensions={0} | all-to-all | bytes 1572864 | tf_op jit(solution)/shard_map/all_to_all | solution.py:437
  116.6 6.7 %multiply_convert_fusion = (bf16[1024,1536]{1,0:T(8,128)(2,1)S(1)}, f32[1024,1536]{1,0:T(8,128)}) fusion(bf16[1024,768]{1,0:T(8,128)(2,1)} %bitcast.124, bf16[1,768,1536]{2,1,0:T(8,128)(2,1)S(1)} %copy-done), kind=kOutput, calls=%fused_computation.9 | convolution fusion | flops 2430074880 | bytes 13369344 | tf_op jit(solution)/shard_map/dot_general | solution.py:367
  123.4 1.7 copy-done.54
  125.0 3.7 %fusion.18 = bf16[32,32,768]{2,1,0:T(8,128)(2,1)} fusion(bf16[32,32,1536]{2,1,0:T(8,128)(2,1)S(1)} %bitcast.143, bf16[1,1536,768]{2,1,0:T(8,128)(2,1)S(1)} %copy-done.51), kind=kOutput, calls=%fused_computation.30 | convolution fusion | flops 2416705536 | bytes 7077888 | tf_op jit(solution)/shard_map/dot_general | solution.py:367
  129.0 8.4 %fusion.6 = bf16[1024,1536]{1,0:T(8,128)(2,1)S(1)} fusion(f32[1024,1536]{1,0:T(8,128)} %get-tuple-element.53, bf16[1024,768]{1,0:T(8,128)(2,1)} %bitcast.140, bf16[1,1536,768]{2,1,0:T(8,128)(2,1)} %param.27), kind=kOutput, calls=%fused_computation.8 | convolution fusion | flops 2447376384 | bytes 13369344 | tf_op jit(solution)/shard_map/dot_general | solution.py:373
  137.4 1.7 copy-done.17
  139.0 3.8 %fusion.21 = bf16[32,32,768]{2,1,0:T(8,128)(2,1)} fusion(bf16[32,32,1536]{2,1,0:T(8,128)(2,1)S(1)} %bitcast.123, bf16[1,768,1536]{2,1,0:T(8,128)(2,1)S(1)} %copy-done), kind=kOutput, calls=%fused_computation.31 | convolution fusion | flops 2416705536 | bytes 7077888 | tf_op jit(solution)/shard_map/dot_general | solution.py:373
  142.9 4.3 %all-to-all-start.1 = ((bf16[16,32,768]{2,1,0:T(8,128)(2,1)}), bf16[16,32,768]{2,1,0:T(8,128)(2,1)}, u32[]{:S(2)}, u32[]{:S(2)}) async-start(bf16[16,32,768]{2,1,0:T(8,128)(2,1)} %reduce-scatter.4.cloned.1.call-done), calls=%async_computation.2 | async-start | bytes 1572864 | tf_op jit(solution)/shard_map/all_to_all | solution.py:447
  147.3 2.5 reduce-scatter.6.cloned.1.call-done
  149.8 16.0 %all-to-all-done.1 = bf16[16,32,768]{2,1,0:T(8,128)(2,1)} async-done(((bf16[16,32,768]{2,1,0:T(8,128)(2,1)}), bf16[16,32,768]{2,1,0:T(8,128)(2,1)}, u32[]{:S(2)}, u32[]{:S(2)}) %all-to-all-start.1) | async-done | bytes 786464 | tf_op jit(solution)/shard_map/all_to_all | solution.py:447
  165.8 4.6 %all-to-all-start.3 = ((bf16[16,32,768]{2,1,0:T(8,128)(2,1)}), bf16[16,32,768]{2,1,0:T(8,128)(2,1)}, u32[]{:S(2)}, u32[]{:S(2)}) async-start(bf16[16,32,768]{2,1,0:T(8,128)(2,1)} %reduce-scatter.6.cloned.1.call-done), calls=%async_computation.5 | async-start | bytes 1572864 | tf_op jit(solution)/shard_map/all_to_all | solution.py:447
  170.4 2.4 fusion.27
  172.9 1.4 fusion.89
  174.3 14.7 %all-to-all-done.3 = bf16[16,32,768]{2,1,0:T(8,128)(2,1)} async-done(((bf16[16,32,768]{2,1,0:T(8,128)(2,1)}), bf16[16,32,768]{2,1,0:T(8,128)(2,1)}, u32[]{:S(2)}, u32[]{:S(2)}) %all-to-all-start.3) | async-done | bytes 786464 | tf_op jit(solution)/shard_map/all_to_all | solution.py:447
  189.0 2.3 multiply_reduce_fusion
  191.4 2.3 convert_add_fusion.1
  194.3 9.6 %attend_backward.1 = (bf16[256,768]{1,0:T(8,128)(2,1)S(1)}, bf16[512,768]{1,0:T(8,128)(2,1)S(1)}, bf16[512,768]{1,0:T(8,128)(2,1)S(1)}, f32[12,8,768]{2,1,0:T(8,128)S(1)}) custom-call(bf16[256,768]{1,0:T(8,128)(2,1)S(1)} %convolution_convert_fusion.7.q_ref, bf16[512,1536]{1,0:T(8,128)(2,1)S(1)} %copy-done.3, bf16[512,1536]{1,0:T(8,128)(2,1)S(1)} %copy-done.3, ...), custom_call_target="tpu_custom_call" | custom-call | flops 805306368 | bytes 9437184 | tf_op jit(solution)/shard_map/attend_backward/pallas_call | solution.py:160
  204.6 1.3 pad_maximum_fusion.1
  206.6 6.9 %convolution_bitcast_fusion = f32[1,1536,768]{2,1,0:T(8,128)} fusion(bf16[1024,1536]{1,0:T(8,128)(2,1)} %copy-done.54, bf16[1024,768]{1,0:T(8,128)(2,1)S(1)} %bitcast.141), kind=kOutput, calls=%fused_computation.10 | convolution fusion | flops 2415919104 | bytes 9437184 | tf_op jit(solution)/shard_map/dot_general | solution.py:370
  213.5 4.4 %convolution_bitcast_fusion.1 = f32[1,768,1536]{2,1,0:T(8,128)} fusion(bf16[1024,768]{1,0:T(8,128)(2,1)S(1)} %bitcast.125, bf16[1024,1536]{1,0:T(8,128)(2,1)S(1)} %copy-done.18), kind=kOutput, calls=%fused_computation.11 | convolution fusion | flops 2415919104 | bytes 9437184 | tf_op jit(solution)/shard_map/dot_general | solution.py:370
  220.2 1.8 convolution_convert_fusion.8
  224.6 1.5 convolution_convert_fusion.2
  226.2 2.2 constant_dynamic-update-slice_fusion
  228.4 2.3 convolution_convert_fusion
  230.7 3.3 %fusion.37 = (bf16[768]{0:T(1024)(128)(2,1)S(1)}, f32[256]{0:T(256)S(1)}, f32[256,768]{1,0:T(8,128)}) fusion(bf16[256,768]{1,0:T(8,128)(2,1)S(1)} %copy-done.14, f32[256]{0:T(256)S(1)} %copy-done.44, f32[768]{0:T(1024)S(1)} %copy-done.28, bf16[256,2304]{1,0:T(8,128)(2,1)} %constant_dynamic-update-slice_fusion, bf16[768,2304]{1,0:T(8,128)(2,1)S(1)} %copy-done.50), kind=kOutput, calls=%fused_computation.60 | convolution fusion | flops 907344896 | bytes 5904896 | tf_op jit(solution)/shard_map/dot_general | solution.py:373
  235.0 2.5 convolution_convert_fusion.3
  237.6 5.4 %concatenate.102.second_ref = bf16[2,8,48,1664]{3,2,1,0:T(8,128)(2,1)} concatenate(bf16[2,8,48,640]{3,2,1,0:T(8,128)(2,1)} %bitcast.126, bf16[2,8,48,768]{3,2,1,0:T(8,128)(2,1)} %bitcast.113, bf16[2,8,48,16]{3,2,1,0:T(8,128)(2,1)} %bitcast.127, bf16[2,8,48,1]{3,2,1,0:T(8,128)(2,1)} %convert_element_type.248, bf16[2,8,48,1]{3,2,1,0:T(8,128)(2,1)} %convert_element_type.249, ...), dimensions={3} | concatenate | bytes 5111808 | tf_op jit(solution)/shard_map/concatenate | solution.py:500
  243.0 1.7 copy-done.4
  244.7 63.1 %sum_over_all.1 = (f32[8,48,1664]{2,1,0:T(8,128)S(1)}, f32[8,48,1664]{2,1,0:T(8,128)S(1)}) custom-call(bf16[2,8,48,1664]{3,2,1,0:T(8,128)(2,1)S(1)} %bitcast.102, bf16[2,8,48,1664]{3,2,1,0:T(8,128)(2,1)S(1)} %copy-done.4), custom_call_target="tpu_custom_call" | custom-call | tf_op jit(solution)/shard_map/sum_over_all/pallas_call | solution.py:317
  307.8 1.1 slice.302
  312.6 3.9 %fusion.121 = (f32[384,768]{1,0:T(8,128)}, f32[384,768]{1,0:T(8,128)}, f32[384,768]{1,0:T(8,128)}) fusion(f32[384,1664]{1,0:T(8,128)} %bitcast.111, f32[384,640]{1,0:T(8,128)} %slice.302, f32[384,128]{1,0:T(8,128)S(1)} %slice.301), kind=kLoop, calls=%fused_computation.185 | loop fusion | flops 294912 | bytes 7077888 | tf_op jit(solution)/shard_map/slice | solution.py:526
  316.5 1.1 fusion.34
  (217 shorter events, 20.2 us)
Async XLA Ops:
  7.2 109.4 %copy-start = (bf16[1,768,1536]{2,1,0:T(8,128)(2,1)S(1)}, bf16[1,768,1536]{2,1,0:T(8,128)(2,1)}, u32[]{:S(2)}) copy-start(bf16[1,768,1536]{2,1,0:T(8,128)(2,1)} %param.26) | copy-start | bytes 7077892
  7.2 5.2 %copy-start.13 = (bf16[256,768]{1,0:T(8,128)(2,1)S(1)}, bf16[256,768]{1,0:T(8,128)(2,1)}, u32[]{:S(2)}) copy-start(bf16[256,768]{1,0:T(8,128)(2,1)} %param.14) | copy-start | bytes 1179652
  7.2 18.5 %all-gather.6.cloned.1.call-start = ((), (), s32[]{:S(2)}) async-start(), calls=%async_computation.7 | async-start | bytes 5308416 | tf_op jit(solution)/shard_map/all_gather | solution.py:381
  10.2 30.1 %all-gather.8.cloned.1.call-start = ((), (), s32[]{:S(2)}) async-start(), calls=%async_computation.8 | async-start | bytes 2359296 | tf_op jit(solution)/shard_map/all_gather | solution.py:398
  12.4 17.5 %copy-start.23 = (bf16[768,19]{0,1:T(8,128)(2,1)}, bf16[768,19]{0,1:T(8,128)(2,1)S(1)}, u32[]{:S(2)}) copy-start(bf16[768,19]{0,1:T(8,128)(2,1)S(1)} %all_gather.18) | copy-start | bytes 87556
  12.5 21.3 %copy-start.27 = (f32[768]{0:T(1024)}, f32[768]{0:T(1024)S(1)}, u32[]{:S(2)}) copy-start(f32[768]{0:T(1024)S(1)} %get-tuple-element.35) | copy-start | bytes 9220
  12.5 47.7 %copy-start.25 = (f32[768]{0:T(1024)}, f32[768]{0:T(1024)S(1)}, u32[]{:S(2)}) copy-start(f32[768]{0:T(1024)S(1)} %get-tuple-element.34) | copy-start | bytes 9220
  13.2 20.6 %copy-start.43 = (f32[256]{0:T(256)}, f32[256]{0:T(256)S(1)}, u32[]{:S(2)}) copy-start(f32[256]{0:T(256)S(1)} %get-tuple-element.47) | copy-start | bytes 3076
  29.2 4.4 %copy-start.36 = (s32[256,1]{0,1:T(1,128)S(1)}, s32[256,1]{0,1:T(1,128)}, u32[]{:S(2)}) copy-start(s32[256,1]{0,1:T(1,128)} %param.17) | copy-start | bytes 3076
  29.2 27.7 %all-gather.10.cloned.1.call-start = ((), (), s32[]{:S(2)}) async-start(), calls=%async_computation.9 | async-start | bytes 1769472 | tf_op jit(solution)/shard_map/all_gather | solution.py:384
  33.8 26.4 %copy-start.31 = (s32[256,1]{0,1:T(1,128)}, s32[256,1]{0,1:T(1,128)S(1)}, u32[]{:S(2)}) copy-start(s32[256,1]{0,1:T(1,128)S(1)} %multiply_add_fusion) | copy-start | bytes 3076
  59.6 30.3 %copy-start.16 = (bf16[256,768]{1,0:T(8,128)(2,1)S(1)}, bf16[256,768]{1,0:T(8,128)(2,1)}, u32[]{:S(2)}) copy-start(bf16[256,768]{1,0:T(8,128)(2,1)} %param.15) | copy-start | bytes 1179652
  62.8 27.0 %all-to-all-start = ((bf16[16,32,768]{2,1,0:T(8,128)(2,1)}), bf16[16,32,768]{2,1,0:T(8,128)(2,1)}, u32[]{:S(2)}, u32[]{:S(2)}) async-start(bf16[16,32,768]{2,1,0:T(8,128)(2,1)} %bitcast.121), calls=%async_computation | async-start | bytes 1572864 | tf_op jit(solution)/shard_map/all_to_all | solution.py:437
  69.7 46.9 %all-gather.12.cloned.1.call-start = ((), (), s32[]{:S(2)}) async-start(), calls=%async_computation.10 | async-start | bytes 2359296 | tf_op jit(solution)/shard_map/all_gather | solution.py:438
  89.8 39.1 %all-gather.14.cloned.1.call-start = ((), (), s32[]{:S(2)}) async-start(), calls=%async_computation.12 | async-start | bytes 2359296 | tf_op jit(solution)/shard_map/all_gather | solution.py:438
  116.5 26.4 %reduce-scatter.4.cloned.1.call-start = ((), (), s32[]{:S(2)}) async-start(), calls=%async_computation.11 | async-start | bytes 2359296 | tf_op jit(solution)/shard_map/reduce_scatter | solution.py:441
  116.6 8.4 %copy-start.51 = (bf16[1,1536,768]{2,1,0:T(8,128)(2,1)S(1)}, bf16[1,1536,768]{2,1,0:T(8,128)(2,1)}, u32[]{:S(2)}) copy-start(bf16[1,1536,768]{2,1,0:T(8,128)(2,1)} %param.27) | copy-start | bytes 7077892
  128.7 21.1 %reduce-scatter.6.cloned.1.call-start = ((), (), s32[]{:S(2)}) async-start(), calls=%async_computation.13 | async-start | bytes 2359296 | tf_op jit(solution)/shard_map/reduce_scatter | solution.py:441
  142.8 27.6 %copy-start.32 = (s32[256,1]{0,1:T(1,128)S(1)}, s32[256,1]{0,1:T(1,128)}, u32[]{:S(2)}) copy-start(s32[256,1]{0,1:T(1,128)} %copy-done.31) | copy-start | bytes 3076
  142.8 30.0 %copy-start.24 = (bf16[768,19]{0,1:T(8,128)(2,1)S(1)}, bf16[768,19]{0,1:T(8,128)(2,1)}, u32[]{:S(2)}) copy-start(bf16[768,19]{0,1:T(8,128)(2,1)} %copy-done.23) | copy-start | bytes 87556
  142.9 30.0 %copy-start.34 = (f32[256]{0:T(256)S(1)}, f32[256]{0:T(256)}, u32[]{:S(2)}) copy-start(f32[256]{0:T(256)} %copy-done.33) | copy-start | bytes 3076
  142.9 30.0 %copy-start.35 = (f32[256]{0:T(256)S(1)}, f32[256]{0:T(256)}, u32[]{:S(2)}) copy-start(f32[256]{0:T(256)} %multiply_reduce_fusion.3) | copy-start | bytes 3076
  142.9 30.0 %copy-start.37 = (s32[256,1]{0,1:T(1,128)S(1)}, s32[256,1]{0,1:T(1,128)}, u32[]{:S(2)}) copy-start(s32[256,1]{0,1:T(1,128)} %param.17) | copy-start | bytes 3076
  142.9 30.0 %copy-start.39 = (f32[256]{0:T(256)S(1)}, f32[256]{0:T(256)}, u32[]{:S(2)}) copy-start(f32[256]{0:T(256)} %copy-done.38) | copy-start | bytes 3076
  142.9 22.8 %all-to-all-start.1 = ((bf16[16,32,768]{2,1,0:T(8,128)(2,1)}), bf16[16,32,768]{2,1,0:T(8,128)(2,1)}, u32[]{:S(2)}, u32[]{:S(2)}) async-start(bf16[16,32,768]{2,1,0:T(8,128)(2,1)} %reduce-scatter.4.cloned.1.call-done), calls=%async_computation.2 | async-start | bytes 1572864 | tf_op jit(solution)/shard_map/all_to_all | solution.py:447
  147.2 41.8 %copy-start.26 = (f32[768]{0:T(1024)S(1)}, f32[768]{0:T(1024)}, u32[]{:S(2)}) copy-start(f32[768]{0:T(1024)} %copy-done.25) | copy-start | bytes 9220
  147.2 41.8 %copy-start.30 = (f32[256]{0:T(256)S(1)}, f32[256]{0:T(256)}, u32[]{:S(2)}) copy-start(f32[256]{0:T(256)} %copy-done.29) | copy-start | bytes 3076
  165.8 28.5 %slice-start = ((s8[6291456]{0:T(1024)(128)(4,1)}), s8[2097152]{0:T(1024)(128)(4,1)S(1)}, s32[]{:S(2)}) async-start(s8[6291456]{0:T(1024)(128)(4,1)} %bitcast.103), calls=%async_computation.15 | async-start | bytes 4194304
  165.8 23.2 %all-to-all-start.3 = ((bf16[16,32,768]{2,1,0:T(8,128)(2,1)}), bf16[16,32,768]{2,1,0:T(8,128)(2,1)}, u32[]{:S(2)}, u32[]{:S(2)}) async-start(bf16[16,32,768]{2,1,0:T(8,128)(2,1)} %reduce-scatter.6.cloned.1.call-done), calls=%async_computation.5 | async-start | bytes 1572864 | tf_op jit(solution)/shard_map/all_to_all | solution.py:447
  170.4 55.8 %reduce-scatter.8.cloned.1.call-start = ((), (), s32[]{:S(2)}) async-start(), calls=%async_computation.14 | async-start | bytes 2359296 | tf_op jit(solution)/shard_map/reduce_scatter | solution.py:478
  170.4 20.9 %copy-start.47 = (f32[256]{0:T(256)S(1)}, f32[256]{0:T(256)}, u32[]{:S(2)}) copy-start(f32[256]{0:T(256)} %get-tuple-element.48) | copy-start | bytes 3076
  189.0 5.2 %slice-start.1 = ((s8[6291456]{0:T(1024)(128)(4,1)}), s8[4194304]{0:T(1024)(128)(4,1)S(1)}, s32[]{:S(2)}) async-start(s8[6291456]{0:T(1024)(128)(4,1)} %bitcast.103), calls=%async_computation.16 | async-start | bytes 8388608
  193.7 10.1 %copy-start.10 = (f32[256,768]{1,0:T(8,128)}, f32[256,768]{1,0:T(8,128)S(1)}, u32[]{:S(2)}) copy-start(f32[256,768]{1,0:T(8,128)S(1)} %get-tuple-element.38) | copy-start | bytes 2359300
  206.6 6.9 %copy-start.18 = (bf16[1024,1536]{1,0:T(8,128)(2,1)S(1)}, bf16[1024,1536]{1,0:T(8,128)(2,1)}, u32[]{:S(2)}) copy-start(bf16[1024,1536]{1,0:T(8,128)(2,1)} %copy-done.17) | copy-start | bytes 9437188
  206.6 6.9 %copy-start.20 = (bf16[32,32,768]{2,1,0:T(8,128)(2,1)S(1)}, bf16[32,32,768]{2,1,0:T(8,128)(2,1)}, u32[]{:S(2)}) copy-start(bf16[32,32,768]{2,1,0:T(8,128)(2,1)} %all-gather.12.cloned.1.call-done) | copy-start | bytes 4718596
  213.5 4.4 %copy-start.9 = (f32[12,8,768]{2,1,0:T(8,128)S(1)}, f32[12,8,768]{2,1,0:T(8,128)}, u32[]{:S(2)}) copy-start(f32[12,8,768]{2,1,0:T(8,128)} %copy-done.8) | copy-start | bytes 884740
  213.5 5.1 %copy-start.41 = (s32[768]{0:T(1024)S(1)}, s32[768]{0:T(1024)}, u32[]{:S(2)}) copy-start(s32[768]{0:T(1024)} %copy-done.40) | copy-start | bytes 9220
  217.8 6.8 %copy-start.11 = (f32[256,768]{1,0:T(8,128)S(1)}, f32[256,768]{1,0:T(8,128)}, u32[]{:S(2)}) copy-start(f32[256,768]{1,0:T(8,128)} %copy-done.10) | copy-start | bytes 2359300
  222.0 6.4 %copy-start.28 = (f32[768]{0:T(1024)S(1)}, f32[768]{0:T(1024)}, u32[]{:S(2)}) copy-start(f32[768]{0:T(1024)} %copy-done.27) | copy-start | bytes 9220
  222.0 6.4 %copy-start.44 = (f32[256]{0:T(256)S(1)}, f32[256]{0:T(256)}, u32[]{:S(2)}) copy-start(f32[256]{0:T(256)} %copy-done.43) | copy-start | bytes 3076
  226.2 4.5 %copy-start.14 = (bf16[256,768]{1,0:T(8,128)(2,1)S(1)}, bf16[256,768]{1,0:T(8,128)(2,1)}, u32[]{:S(2)}) copy-start(bf16[256,768]{1,0:T(8,128)(2,1)} %param.14) | copy-start | bytes 1179652
  226.2 4.5 %copy-start.50 = (bf16[768,2304]{1,0:T(8,128)(2,1)S(1)}, bf16[768,2304]{1,0:T(8,128)(2,1)}, u32[]{:S(2)}) copy-start(bf16[768,2304]{1,0:T(8,128)(2,1)} %all-gather.6.cloned.1.call-done) | copy-start | bytes 10616836
  234.0 3.6 %copy-start.21 = (bf16[2,8,48,1]{3,2,1,0:T(8,128)(2,1)S(1)}, bf16[2,8,48,1]{3,2,1,0:T(8,128)(2,1)}, u32[]{:S(2)}) copy-start(bf16[2,8,48,1]{3,2,1,0:T(8,128)(2,1)} %convert_element_type.250) | copy-start | bytes 4612
  307.8 3.3 %copy-start.6 = (f32[8,48,1664]{2,1,0:T(8,128)}, f32[8,48,1664]{2,1,0:T(8,128)S(1)}, u32[]{:S(2)}) copy-start(f32[8,48,1664]{2,1,0:T(8,128)S(1)} %get-tuple-element.26) | copy-start | bytes 7667716
  312.6 4.0 %copy-start.12 = (f32[256,768]{1,0:T(8,128)S(1)}, f32[256,768]{1,0:T(8,128)}, u32[]{:S(2)}) copy-start(f32[256,768]{1,0:T(8,128)} %copy-done.10) | copy-start | bytes 2359300
  312.6 4.0 %copy-start.22 = (f32[256,768]{1,0:T(8,128)S(1)}, f32[256,768]{1,0:T(8,128)}, u32[]{:S(2)}) copy-start(f32[256,768]{1,0:T(8,128)} %get-tuple-element.59) | copy-start | bytes 2359300
  312.6 4.0 %copy-start.45 = (f32[256]{0:T(256)S(1)}, f32[256]{0:T(256)}, u32[]{:S(2)}) copy-start(f32[256]{0:T(256)} %get-tuple-element.46) | copy-start | bytes 3076
  312.6 5.1 %copy-start.1 = (bf16[1,768,1536]{2,1,0:T(8,128)(2,1)S(1)}, bf16[1,768,1536]{2,1,0:T(8,128)(2,1)}, u32[]{:S(2)}) copy-start(bf16[1,768,1536]{2,1,0:T(8,128)(2,1)} %param.26) | copy-start | bytes 7077892
  (20 other events, 40.0 us)
Sparse Core Ops, SparseCore 0:
  10.3 15.3 all-gather.5
  29.3 10.9 all-gather.7
  41.9 10.4 all-gather.9
  89.9 9.2 all-gather.11
  116.6 7.5 all-gather.13
  128.8 8.2 reduce-scatter.3
  143.0 6.7 reduce-scatter.5
  206.0 8.3 reduce-scatter.7
